TPU v7x, 128 devices: a whole 4x4x4 slice. The times are simulated.
128 devices in a mesh: gx: 8 (over z_lo, x), gy: 16 (over z_hi, y, core).
Axes of the slice: x: 4, y: 4, z: 4 (z_hi: 2, z_lo: 2; z = z_hi * 2 + z_lo), core: 2. Of those that a mesh axis runs over, the one named last changes fastest.
Arguments:
- source: float32 [2, 1024, 64, 512], P(None, ('gx', 'gy')), may hold values from -6 to 6
- weights: float32 [7, 2, 1024, 64, 128], P(None, None, ('gx', 'gy')), may hold values from -0.375 to 0.375
- interp: float32 [2, 1024, 64, 128], P(None, ('gx', 'gy')), may hold values from -0.5 to 0.5
Outputs:
- far_field: float32 [2, 512, 1024, 128], P(None, ('gx', 'gy'))
All inputs are finite; a program needn't handle non-finite values.
Results may differ from a plain program's by a relative error of at most 0.0001.
Values sent between devices are 32-bit elements; how exact they have to be, the bound alone decides.
No kernel may reach another device: no remote copies, remote signals or barrier semaphores. Data moves between devices by JAX's collectives and lax.ppermute only.
A program may use at most 64 MiB of HBM per device.

v0:
```python
import jax
import jax.numpy as jnp
from jax import lax
from jax.sharding import PartitionSpec as P


def from_partner(value, axis, apart):
    mask = 2**apart
    pairs = [(source, source ^ mask) for source in range(lax.axis_size(axis))]
    return lax.ppermute(value, axis, pairs)


def cmul(blocks, coeffs):

    def one(a, b):
        return jnp.einsum("krj,kjs->krs", a, b, precision=lax.Precision.HIGHEST)

    real = one(blocks[0], coeffs[0]) - one(blocks[1], coeffs[1])
    imag = one(blocks[0], coeffs[1]) + one(blocks[1], coeffs[0])
    return jnp.stack([real, imag])


def on_device(source, weights, interp):
    rank = source.shape[2]
    bits_gy = lax.axis_size("gy").bit_length() - 1
    bits_gx = lax.axis_size("gx").bit_length() - 1
    state = source
    for level in range(bits_gy + bits_gx):
        blocks = weights[level]
        if level < bits_gy:
            my_bit = lax.axis_index("gy") >> level & 1
        else:
            my_bit = lax.axis_index("gx") >> level - bits_gy & 1
        first = blocks[..., :rank]
        second = blocks[..., rank:]
        own_block = jnp.where(my_bit == 0, first, second)
        other_block = jnp.where(my_bit == 0, second, first)
        own_term = cmul(own_block, state)
        if level < bits_gy:
            partner = from_partner(state, "gy", level)
        else:
            partner = from_partner(state, "gx", level - bits_gy)
        state = own_term + cmul(other_block, partner)

    def proj(a, b):
        return jnp.einsum("krq,krs->skq", a, b, precision=lax.Precision.HIGHEST)

    real = proj(interp[0], state[0]) - proj(interp[1], state[1])
    imag = proj(interp[0], state[1]) + proj(interp[1], state[0])
    samples = jnp.stack([real, imag])
    result = lax.all_to_all(samples, ("gx", "gy"), split_axis=1, concat_axis=2, tiled=True)
    return result


def solution(mesh):
    return jax.shard_map(
        on_device,
        mesh=mesh,
        in_specs=(
            P(None, ("gx", "gy"), None, None),
            P(None, None, ("gx", "gy"), None, None),
            P(None, ("gx", "gy"), None, None),
        ),
        out_specs=P(None, ("gx", "gy"), None, None),
        check_vma=False,
    )
```

profile of v0, /device:TPU:1, one launch (start us, length us, event | category | flops | bytes accessed | tf_op | source)
XLA Modules:
  0.0 440.3 jit_solution(3669775536634256674)
XLA Ops:
  0.0 1.4 collective-permute-start
  1.4 3.6 slice_bitcast_fusion.90
  5.2 1.4 copy-done
  7.6 1.0 fusion.26
  9.6 1.0 fusion.27
  12.6 1.0 fusion.24
  13.6 1.0 fusion.25
  15.1 1.9 collective-permute-start.1
  17.0 1.4 slice_select_fusion.2
  19.4 1.0 fusion.22
  21.4 1.0 fusion.23
  22.4 40.6 %collective-permute-done.1 = f32[2,8,64,512]{3,2,1,0:T(8,128)} collective-permute-done((f32[2,8,64,512]{3,2,1,0:T(8,128)S(1)}, f32[2,8,64,512]{3,2,1,0:T(8,128)}, u32[]{:S(2)}, u32[]{:S(2)}) %collective-permute-start.1) | collective-permute-done | bytes 2097184 | tf_op jit(solution)/shard_map/ppermute | solution.py:10
  63.0 2.2 fusion.38
  65.2 2.2 fusion.39
  67.4 2.2 fusion.20
  69.6 2.2 fusion.21
  72.3 3.3 collective-permute-start.2
  75.6 1.4 slice_select_fusion.4
  78.0 1.0 fusion.18
  80.0 1.0 fusion.19
  81.0 39.7 %collective-permute-done.2 = f32[2,8,64,512]{3,2,1,0:T(8,128)} collective-permute-done((f32[2,8,64,512]{3,2,1,0:T(8,128)S(1)}, f32[2,8,64,512]{3,2,1,0:T(8,128)}, u32[]{:S(2)}, u32[]{:S(2)}) %collective-permute-start.2) | collective-permute-done | bytes 2097184 | tf_op jit(solution)/shard_map/ppermute | solution.py:10
  120.6 2.2 fusion.42
  122.8 2.2 fusion.43
  125.1 2.2 fusion.16
  127.3 2.2 fusion.17
  130.0 3.9 collective-permute-start.3
  133.9 1.4 slice_select_fusion.6
  136.3 1.0 fusion.14
  138.3 1.0 fusion.15
  139.3 39.0 %collective-permute-done.3 = f32[2,8,64,512]{3,2,1,0:T(8,128)} collective-permute-done((f32[2,8,64,512]{3,2,1,0:T(8,128)S(1)}, f32[2,8,64,512]{3,2,1,0:T(8,128)}, u32[]{:S(2)}, u32[]{:S(2)}) %collective-permute-start.3) | collective-permute-done | bytes 2097184 | tf_op jit(solution)/shard_map/ppermute | solution.py:10
  178.3 2.2 fusion.46
  180.5 2.2 fusion.47
  182.7 2.2 fusion.12
  184.9 2.2 fusion.13
  187.6 1.5 collective-permute-start.4
  189.2 1.4 slice_select_fusion.8
  191.6 1.0 fusion.10
  193.6 1.0 fusion.11
  194.6 38.3 %collective-permute-done.4 = f32[2,8,64,512]{3,2,1,0:T(8,128)} collective-permute-done((f32[2,8,64,512]{3,2,1,0:T(8,128)S(1)}, f32[2,8,64,512]{3,2,1,0:T(8,128)}, u32[]{:S(2)}, u32[]{:S(2)}) %collective-permute-start.4) | collective-permute-done | bytes 2097184 | tf_op jit(solution)/shard_map/ppermute | solution.py:10
  232.9 2.2 fusion.50
  235.1 2.2 fusion.51
  237.3 2.2 fusion.8
  239.5 2.2 fusion.9
  242.2 3.3 collective-permute-start.5
  246.7 1.0 fusion.6
  248.7 1.0 fusion.7
  249.7 38.5 %collective-permute-done.5 = f32[2,8,64,512]{3,2,1,0:T(8,128)} collective-permute-done((f32[2,8,64,512]{3,2,1,0:T(8,128)S(1)}, f32[2,8,64,512]{3,2,1,0:T(8,128)}, u32[]{:S(2)}, u32[]{:S(2)}) %collective-permute-start.5) | collective-permute-done | bytes 2097184 | tf_op jit(solution)/shard_map/ppermute | solution.py:10
  288.3 2.2 fusion.54
  290.5 2.2 fusion.55
  292.7 2.2 fusion.4
  294.9 2.2 fusion.5
  299.3 1.0 fusion.2
  302.3 38.7 %collective-permute-done.6 = f32[2,8,64,512]{3,2,1,0:T(8,128)} collective-permute-done((f32[2,8,64,512]{3,2,1,0:T(8,128)S(1)}, f32[2,8,64,512]{3,2,1,0:T(8,128)}, u32[]{:S(2)}, u32[]{:S(2)}) %collective-permute-start.6) | collective-permute-done | bytes 2097184 | tf_op jit(solution)/shard_map/ppermute | solution.py:10
  341.0 2.2 fusion.58
  343.2 2.2 fusion.59
  345.4 2.2 fusion
  347.6 2.2 fusion.1
  350.9 3.5 fusion.61
  354.3 3.7 fusion.60
  358.0 3.5 add_bitcast_fusion
  361.5 3.5 subtract_bitcast_fusion
  365.4 2.4 copy.5
  367.8 70.0 %all_to_all.18 = f32[2,512,8,128]{3,2,0,1:T(8,128)S(1)} all-to-all(f32[2,512,8,128]{3,2,0,1:T(8,128)S(1)} %copy.5), channel_id=1, replica_groups=mesh['gx'=8,'gy'=16] {'gx','gy'}, dimensions={1} | all-to-all | bytes 8388608 | tf_op jit(solution)/shard_map/all_to_all | solution.py:51
  437.8 2.3 copy.8
  (33 shorter events, 22.0 us)
Async XLA Ops:
  0.0 10.6 %collective-permute-start = (f32[2,8,64,512]{3,2,1,0:T(8,128)}, f32[2,8,64,512]{3,2,1,0:T(8,128)S(1)}, u32[]{:S(2)}, u32[]{:S(2)}) collective-permute-start(f32[2,8,64,512]{3,2,1,0:T(8,128)} %param.3), channel_id=1, source_target_pairs={{0,1},{1,0},{2,3},{3,2},{4,5},{5,4},{6,7},{7,6},{8,9},{9,8},{10,11... | collective-permute-start | bytes 6291464 | tf_op jit(solution)/shard_map/ppermute | solution.py:10
  5.0 1.6 copy-start
  15.1 47.9 %collective-permute-start.1 = (f32[2,8,64,512]{3,2,1,0:T(8,128)S(1)}, f32[2,8,64,512]{3,2,1,0:T(8,128)}, u32[]{:S(2)}, u32[]{:S(2)}) collective-permute-start(f32[2,8,64,512]{3,2,1,0:T(8,128)S(1)} %maximum_add_fusion), channel_id=1, source_target_pairs={{0,2},{1,3},{2,0},{3,1},{4,6},{5,7},{6,4},{7,5},{8,10},{9,11},{10,... | collective-permute-start | bytes 6291464 | tf_op jit(solution)/shard_map/ppermute | solution.py:10
  72.3 48.3 %collective-permute-start.2 = (f32[2,8,64,512]{3,2,1,0:T(8,128)S(1)}, f32[2,8,64,512]{3,2,1,0:T(8,128)}, u32[]{:S(2)}, u32[]{:S(2)}) collective-permute-start(f32[2,8,64,512]{3,2,1,0:T(8,128)S(1)} %maximum_add_fusion.1), channel_id=1, source_target_pairs={{0,4},{1,5},{2,6},{3,7},{4,0},{5,1},{6,2},{7,3},{8,12},{9,13},{10,... | collective-permute-start | bytes 6291464 | tf_op jit(solution)/shard_map/ppermute | solution.py:10
  130.0 48.3 %collective-permute-start.3 = (f32[2,8,64,512]{3,2,1,0:T(8,128)S(1)}, f32[2,8,64,512]{3,2,1,0:T(8,128)}, u32[]{:S(2)}, u32[]{:S(2)}) collective-permute-start(f32[2,8,64,512]{3,2,1,0:T(8,128)S(1)} %maximum_add_fusion.2), channel_id=1, source_target_pairs={{0,8},{1,9},{2,10},{3,11},{4,12},{5,13},{6,14},{7,15},{8,0},{9,1},... | collective-permute-start | bytes 6291464 | tf_op jit(solution)/shard_map/ppermute | solution.py:10
  187.6 45.2 %collective-permute-start.4 = (f32[2,8,64,512]{3,2,1,0:T(8,128)S(1)}, f32[2,8,64,512]{3,2,1,0:T(8,128)}, u32[]{:S(2)}, u32[]{:S(2)}) collective-permute-start(f32[2,8,64,512]{3,2,1,0:T(8,128)S(1)} %maximum_add_fusion.3), channel_id=1, source_target_pairs={{0,16},{16,0},{32,48},{48,32},{64,80},{80,64},{96,112},{112,96},{1... | collective-permute-start | bytes 6291464 | tf_op jit(solution)/shard_map/ppermute | solution.py:10
  242.2 46.0 %collective-permute-start.5 = (f32[2,8,64,512]{3,2,1,0:T(8,128)S(1)}, f32[2,8,64,512]{3,2,1,0:T(8,128)}, u32[]{:S(2)}, u32[]{:S(2)}) collective-permute-start(f32[2,8,64,512]{3,2,1,0:T(8,128)S(1)} %maximum_add_fusion.4), channel_id=1, source_target_pairs={{0,32},{16,48},{32,0},{48,16},{64,96},{80,112},{96,64},{112,80},{1... | collective-permute-start | bytes 6291464 | tf_op jit(solution)/shard_map/ppermute | solution.py:10
  297.6 43.3 %collective-permute-start.6 = (f32[2,8,64,512]{3,2,1,0:T(8,128)S(1)}, f32[2,8,64,512]{3,2,1,0:T(8,128)}, u32[]{:S(2)}, u32[]{:S(2)}) collective-permute-start(f32[2,8,64,512]{3,2,1,0:T(8,128)S(1)} %maximum_add_fusion.5), channel_id=1, source_target_pairs={{0,64},{16,80},{32,96},{48,112},{64,0},{80,16},{96,32},{112,48},{1... | collective-permute-start | bytes 6291464 | tf_op jit(solution)/shard_map/ppermute | solution.py:10
  349.8 1.0 copy-start.1
where the time goes:
time: 448 us; the launch traced here: 440 us
  waiting for transfers between devices  235 us (52%)
  matrix products  98.8 us (22%)
  blocking collectives  70 us (16%)
  starting transfers between devices  15.7 us (4%)
  local copies, waits for them, and re-layouts  10.1 us (2%)
  other arithmetic  10.1 us (2%)
    ppermute x7, waiting for transfers between devices, from_partner(): return lax.ppermute(value, axis, pairs)  235 us
    dot_general x56, matrix products, one(): return jnp.einsum('krj,kjs->krs', a, b, precision=lax.Precision.HIGHEST)  84.6 us
    all_to_all x1, blocking collectives, on_device(): lax.all_to_all(samples, ('gx', 'gy'), split_axis=1, concat_axis=2, tiled=...  70 us
    ppermute x7, starting transfers between devices, from_partner(): return lax.ppermute(value, axis, pairs)  15.7 us
    dot_general x4, matrix products, proj(): return jnp.einsum('krq,krs->skq', a, b, precision=lax.Precision.HIGHEST)  14.1 us
  transfers between devices with their start and end apart: 7, of which 6 were waited for; matrix products, arithmetic and copies ran while one was open for 9% of the time, Pallas kernels for 0%

commit v1 on v0

v1 whole, which is shorter than its diff:
```python
import jax
import jax.numpy as jnp
from jax import lax
from jax.experimental import pallas as pl
from jax.experimental.pallas import tpu as pltpu
from jax.sharding import PartitionSpec as P

AXES = ("gx", "gy")
TILE = 256
VMEM_BYTES = 48 * 1024 * 1024


def halves(value):
    high = value.astype(jnp.bfloat16)
    return high, (value - high.astype(jnp.float32)).astype(jnp.bfloat16)


def dot3(a_high, a_low, b_high, b_low):
    rows = a_high.shape[0]
    both = jnp.dot(jnp.concatenate([a_high, a_low], 0), b_high, preferred_element_type=jnp.float32)
    return both[:rows] + both[rows:] + jnp.dot(a_high, b_low, preferred_element_type=jnp.float32)


def real_rows(real, imag):
    return jnp.concatenate([jnp.concatenate([real, -imag], 1), jnp.concatenate([imag, real], 1)], 0)


def first_level_kernel(bit_ref, own_ref, other_ref, w_ref, out_ref):
    swap = bit_ref[0] == 1
    real, imag = w_ref[0, 0, 0], w_ref[0, 1, 0]
    real = jnp.where(swap, pltpu.roll(real, 64, 1), real)
    imag = jnp.where(swap, pltpu.roll(imag, 64, 1), imag)
    block = real_rows(real, imag)
    coeffs = jnp.concatenate([own_ref[0, 0], other_ref[0, 0], own_ref[1, 0], other_ref[1, 0]], 0)
    out_ref[0] = dot3(*halves(block), *halves(coeffs))


def first_level(bit, own, other, weights):
    _, boxes, rank, frames = own.shape
    state = pl.BlockSpec((2, 1, rank, frames), lambda k, bit: (0, k, 0, 0))
    return pl.pallas_call(
        first_level_kernel,
        out_shape=jax.ShapeDtypeStruct((boxes, 2 * rank, frames), jnp.float32),
        grid_spec=pltpu.PrefetchScalarGridSpec(
            num_scalar_prefetch=1,
            grid=(boxes,),
            in_specs=[
                state,
                state,
                pl.BlockSpec((1, 2, 1, rank, 2 * rank), lambda k, bit: (0, 0, k, 0, 0)),
            ],
            out_specs=pl.BlockSpec((1, 2 * rank, frames), lambda k, bit: (k, 0, 0)),
        ),
        compiler_params=pltpu.CompilerParams(vmem_limit_bytes=VMEM_BYTES),
        cost_estimate=pl.CostEstimate(flops=900_000_000, bytes_accessed=7_000_000, transcendentals=0),
        name="first_level",
    )(bit, own, other, weights)


def one_level(state_ref, w_ref, at, mask):
    boxes = state_ref.shape[0]
    rank = state_ref.shape[1] // 2
    for low in range(boxes):
        if low & mask:
            continue
        high = low | mask
        block = jnp.concatenate(
            [real_rows(w_ref[low, at, 0], w_ref[low, at, 1]), real_rows(w_ref[high, at, 0], w_ref[high, at, 1])], 0
        )
        coeffs = jnp.concatenate(
            [state_ref[low, :rank], state_ref[high, :rank], state_ref[low, rank:], state_ref[high, rank:]], 0
        )
        new = dot3(*halves(block), *halves(coeffs))
        state_ref[low] = new[: 2 * rank]
        state_ref[high] = new[2 * rank :]


def three_levels_kernel(in_ref, w_ref, out_ref):
    out_ref[...] = in_ref[...]
    for at in range(3):
        one_level(out_ref, w_ref, at, 1 << at)


def three_levels(state, weights):
    boxes, rows, frames = state.shape
    tile = pl.BlockSpec((boxes, rows, TILE), lambda i: (0, 0, i))
    return pl.pallas_call(
        three_levels_kernel,
        out_shape=jax.ShapeDtypeStruct(state.shape, jnp.float32),
        grid=(frames // TILE,),
        in_specs=[tile, pl.BlockSpec((boxes, 3, 2, rows // 2, rows), lambda i: (0, 0, 0, 0, 0))],
        out_specs=tile,
        compiler_params=pltpu.CompilerParams(vmem_limit_bytes=VMEM_BYTES),
        cost_estimate=pl.CostEstimate(flops=2_700_000_000, bytes_accessed=6_000_000, transcendentals=0),
        name="three_levels",
    )(state, weights)


def last_levels_kernel(in_ref, w_ref, out_ref, state_ref):
    state_ref[...] = in_ref[...]
    for at in range(3):
        one_level(state_ref, w_ref, at, 1 << at)
    boxes = state_ref.shape[0]
    for box in range(boxes):
        real, imag = w_ref[box, 3, 0], w_ref[box, 3, 1]
        block = jnp.concatenate([jnp.concatenate([real, imag], 1), jnp.concatenate([-imag, real], 1)], 0)
        samples = dot3(*halves(jnp.transpose(state_ref[box])), *halves(block))
        columns = real.shape[1]
        count = samples.shape[0]
        out_ref[pl.ds(box, count, stride=2 * boxes), :] = samples[:, :columns]
        out_ref[pl.ds(boxes + box, count, stride=2 * boxes), :] = samples[:, columns:]


def last_levels(state, weights):
    boxes, rows, frames = state.shape
    return pl.pallas_call(
        last_levels_kernel,
        out_shape=jax.ShapeDtypeStruct((frames * 2 * boxes, rows), jnp.float32),
        grid=(frames // TILE,),
        in_specs=[
            pl.BlockSpec((boxes, rows, TILE), lambda i: (0, 0, i)),
            pl.BlockSpec((boxes, 4, 2, rows // 2, rows), lambda i: (0, 0, 0, 0, 0)),
        ],
        out_specs=pl.BlockSpec((TILE * 2 * boxes, rows), lambda i: (i, 0)),
        scratch_shapes=[pltpu.VMEM((boxes, rows, TILE), jnp.float32)],
        compiler_params=pltpu.CompilerParams(vmem_limit_bytes=VMEM_BYTES),
        cost_estimate=pl.CostEstimate(flops=3_600_000_000, bytes_accessed=8_000_000, transcendentals=0),
        name="last_levels",
    )(state, weights)


def on_device(source, weights, interp):
    groups_y = [[g * 16 + h * 2 + c for h in range(8)] for g in range(8) for c in range(2)]

    def swap_y(value):
        return lax.all_to_all(value, AXES, 0, 0, axis_index_groups=groups_y, tiled=True)

    def swap_x(value):
        return lax.all_to_all(value, "gx", 0, 0, tiled=True)

    bit = (lax.axis_index("gy") & 1).astype(jnp.int32).reshape(1)
    other = lax.ppermute(source, "gy", [(i, i ^ 1) for i in range(16)])
    moved = jnp.concatenate([weights[1:], interp[None]], 0).transpose(2, 0, 1, 3, 4)
    moved = swap_y(moved)
    late = swap_x(moved[:, 3:])
    state = first_level(bit, source, other, weights)
    state = swap_y(state)
    state = three_levels(state, moved)
    state = swap_x(state)
    samples = last_levels(state, late)
    samples = samples.reshape(128, -1, samples.shape[-1])
    samples = lax.all_to_all(samples, AXES, 0, 0, tiled=True)
    samples = samples.reshape(8, 8, 2, 4, 2, 8, 128).transpose(4, 3, 5, 0, 2, 1, 6)
    return samples.reshape(2, 4, 1024, 128)


def solution(mesh):
    return jax.shard_map(
        on_device,
        mesh=mesh,
        in_specs=(
            P(None, ("gx", "gy"), None, None),
            P(None, None, ("gx", "gy"), None, None),
            P(None, ("gx", "gy"), None, None),
        ),
        out_specs=P(None, ("gx", "gy"), None, None),
        check_vma=False,
    )
```

time: 448 us -> 240 us (0.54); the launches traced: 440 us -> 239 us
  waiting for transfers between devices: 235 us -> 84.2 us
  matrix products: 98.8 us -> 0 us
  blocking collectives: 70 us -> 93.2 us
  Pallas kernels: 0 us -> 19.9 us
  starting transfers between devices: 15.7 us -> 27.4 us
  other arithmetic: 10.1 us -> 4.21 us
    ppermute x7 -> x1, waiting for transfers between devices: 235 us -> 3.92 us  [on_device(): other = lax.ppermute(source, 'gy', [(i, i ^ 1) for i in range(16)])]
    dot_general x60 -> x0, matrix products: 98.8 us -> none  [the longest x56 84.6 us: one(): return jnp.einsum('krj,kjs->krs', a, b, precision=lax.Precision.HIGHEST)]
    all_to_all x0 -> x3, waiting for transfers between devices: none -> 80.3 us  [the longest x2 59.2 us: swap_y(): lax.all_to_all(value, AXES, 0, 0, axis_index_groups=groups_y, tiled=True)]
    all_to_all x0 -> x3, starting transfers between devices: none -> 26.4 us  [the longest x2 21.9 us: swap_y(): lax.all_to_all(value, AXES, 0, 0, axis_index_groups=groups_y, tiled=True)]
    all_to_all x1 -> x2, blocking collectives: 70 us -> 93.2 us  [the longest x1 65 us: on_device(): samples = lax.all_to_all(samples, AXES, 0, 0, tiled=True)]
    pallas_call x0 -> x3, Pallas kernels: none -> 19.9 us  [the longest x1 8.43 us: last_levels(): pl.pallas_call(last_levels_kernel, out_shape=jax.ShapeDtypeStruct((frames...]
    ppermute x7 -> x1, starting transfers between devices: 15.7 us -> 1.03 us  [on_device(): other = lax.ppermute(source, 'gy', [(i, i ^ 1) for i in range(16)])]
    select_n x7 -> x0, other arithmetic: 6.32 us -> none  [on_device(): other_block = jnp.where(my_bit == 0, second, first)]
  transfers between devices with their start and end apart: 7 -> 4, of which waited for: 6 -> 4; matrix products, arithmetic and copies ran while one was open for 9% -> 1% of each run, Pallas kernels for 0% -> 5%
where the time goes in v1:
time: 240 us; the launch traced here: 239 us
  blocking collectives  93.2 us (39%)
  waiting for transfers between devices  84.2 us (35%)
  starting transfers between devices  27.4 us (11%)
  Pallas kernels  19.9 us (8%)
  local copies, waits for them, and re-layouts  9.99 us (4%)
  other arithmetic  4.21 us (2%)
    all_to_all x1, blocking collectives, on_device(): samples = lax.all_to_all(samples, AXES, 0, 0, tiled=True)  65 us
    all_to_all x2, waiting for transfers between devices, swap_y(): lax.all_to_all(value, AXES, 0, 0, axis_index_groups=groups_y, tiled=True)  59.2 us
    all_to_all x1, blocking collectives, swap_x(): return lax.all_to_all(value, 'gx', 0, 0, tiled=True)  28.1 us
    all_to_all x2, starting transfers between devices, swap_y(): lax.all_to_all(value, AXES, 0, 0, axis_index_groups=groups_y, tiled=True)  21.9 us
    all_to_all x1, waiting for transfers between devices, swap_x(): return lax.all_to_all(value, 'gx', 0, 0, tiled=True)  21.1 us
    pallas_call x1, Pallas kernels, last_levels(): pl.pallas_call(last_levels_kernel, out_shape=jax.ShapeDtypeStruct((frames...  8.43 us
    pallas_call x1, Pallas kernels, first_level(): pl.pallas_call(first_level_kernel, out_shape=jax.ShapeDtypeStruct((boxes,...  6.78 us
  transfers between devices with their start and end apart: 4, of which 4 were waited for; matrix products, arithmetic and copies ran while one was open for 1% of the time, Pallas kernels for 5%

profile of v1, /device:TPU:1, one launch (start us, length us, event | category | flops | bytes accessed | tf_op | source)
XLA Modules:
  0.0 238.9 jit_solution(11107935626116166329)
XLA Ops:
  0.0 1.1 copy.11
  1.1 4.2 %maximum_bitcast_fusion = f32[8,7,2,64,128]{4,3,2,1,0:T(8,128)} fusion(f32[1,2,8,64,128]{4,3,1,0,2:T(8,128)S(1)} %bitcast.13, f32[7,2,8,64,128]{4,3,2,1,0:T(8,128)} %w_ref.1), kind=kLoop, calls=%fused_computation | loop fusion | flops 917504 | bytes 7340032 | tf_op jit(solution)/shard_map/transpose | solution.py:143
  5.3 0.0 copy-start
  5.3 8.5 %all-to-all-start.1 = ((f32[8,7,2,64,128]{4,3,2,1,0:T(8,128)}), f32[8,7,2,64,128]{4,3,2,1,0:T(8,128)}, u32[]{:S(2)}, u32[]{:S(2)}) async-start(f32[8,7,2,64,128]{4,3,2,1,0:T(8,128)} %maximum_bitcast_fusion), calls=%async_computation.1 | async-start | bytes 7340032 | tf_op jit(solution)/shard_map/all_to_all | solution.py:136
  13.8 0.0 copy-done
  13.8 1.0 collective-permute-start
  14.8 3.9 %collective-permute-done.other_ref = f32[2,8,64,512]{3,2,1,0:T(8,128)} collective-permute-done((f32[2,8,64,512]{3,2,1,0:T(8,128)S(1)}, f32[2,8,64,512]{3,2,1,0:T(8,128)}, u32[]{:S(2)}, u32[]{:S(2)}) %collective-permute-start) | collective-permute-done | bytes 2097184 | tf_op jit(solution)/shard_map/ppermute | solution.py:142
  18.7 6.8 %first_level.1 = f32[8,128,512]{2,1,0:T(8,128)} custom-call(s32[1]{0:T(128)} %bitcast.bit_ref, f32[2,8,64,512]{3,2,1,0:T(8,128)S(1)} %copy-done, f32[2,8,64,512]{3,2,1,0:T(8,128)} %collective-permute-done.other_ref, f32[7,2,8,64,128]{4,3,2,1,0:T(8,128)} %w_ref.1), custom_call_target="tpu_custom_call" | custom-call | flops 900000000 | bytes 7000000 | tf_op jit(solution)/shard_map/first_level/pallas_call | solution.py:41
  25.5 33.8 %all-to-all-done.1.w_ref = f32[8,7,2,64,128]{4,3,2,1,0:T(8,128)} async-done(((f32[8,7,2,64,128]{4,3,2,1,0:T(8,128)}), f32[8,7,2,64,128]{4,3,2,1,0:T(8,128)}, u32[]{:S(2)}, u32[]{:S(2)}) %all-to-all-start.1) | async-done | bytes 3670048 | tf_op jit(solution)/shard_map/all_to_all | solution.py:136
  59.3 13.4 %all-to-all-start = ((f32[8,128,512]{2,1,0:T(8,128)}), f32[8,128,512]{2,1,0:T(8,128)S(1)}, u32[]{:S(2)}, u32[]{:S(2)}) async-start(f32[8,128,512]{2,1,0:T(8,128)} %first_level.1), calls=%async_computation | async-start | bytes 4194304 | tf_op jit(solution)/shard_map/all_to_all | solution.py:136
  72.7 3.1 %slice.8 = f32[8,4,2,64,128]{4,3,2,1,0:T(8,128)} slice(f32[8,7,2,64,128]{4,3,2,1,0:T(8,128)} %all-to-all-done.1.w_ref), slice={[0:8], [3:7], [0:2], [0:64], [0:128]} | slice | bytes 4194304 | tf_op jit(solution)/shard_map/slice | solution.py:145
  75.9 25.4 %all-to-all-done.in_ref = f32[8,128,512]{2,1,0:T(8,128)S(1)} async-done(((f32[8,128,512]{2,1,0:T(8,128)}), f32[8,128,512]{2,1,0:T(8,128)S(1)}, u32[]{:S(2)}, u32[]{:S(2)}) %all-to-all-start) | async-done | bytes 2097184 | tf_op jit(solution)/shard_map/all_to_all | solution.py:136
  101.3 4.5 %all-to-all-start.3 = ((f32[8,4,2,64,128]{4,3,2,1,0:T(8,128)}), f32[8,4,2,64,128]{4,3,2,1,0:T(8,128)}, u32[]{:S(2)}, u32[]{:S(2)}) async-start(f32[8,4,2,64,128]{4,3,2,1,0:T(8,128)} %slice.8), calls=%async_computation.3 | async-start | bytes 4194304 | tf_op jit(solution)/shard_map/all_to_all | solution.py:139
  105.7 4.7 %three_levels.1 = f32[8,128,512]{2,1,0:T(8,128)S(1)} custom-call(f32[8,128,512]{2,1,0:T(8,128)S(1)} %all-to-all-done.in_ref, f32[8,7,2,64,128]{4,3,2,1,0:T(8,128)} %all-to-all-done.1.w_ref), custom_call_target="tpu_custom_call" | custom-call | flops 2700000000 | bytes 6000000 | tf_op jit(solution)/shard_map/three_levels/pallas_call | solution.py:87
  110.4 0.0 copy-start.1
  110.5 1.3 copy-done.1
  111.8 21.1 %all-to-all-done.3.w_ref = f32[8,4,2,64,128]{4,3,2,1,0:T(8,128)} async-done(((f32[8,4,2,64,128]{4,3,2,1,0:T(8,128)}), f32[8,4,2,64,128]{4,3,2,1,0:T(8,128)}, u32[]{:S(2)}, u32[]{:S(2)}) %all-to-all-start.3) | async-done | bytes 2097184 | tf_op jit(solution)/shard_map/all_to_all | solution.py:139
  132.9 28.1 %all_to_all.25.in_ref = f32[8,128,512]{2,1,0:T(8,128)S(1)} all-to-all(f32[8,128,512]{2,1,0:T(8,128)} %copy-done.1), channel_id=1, replica_groups=mesh['gx'=8,'gy'=16] {'gx'}, dimensions={0} | all-to-all | bytes 4194304 | tf_op jit(solution)/shard_map/all_to_all | solution.py:139
  161.0 8.4 %last_levels.1 = f32[8192,128]{1,0:T(8,128)} custom-call(f32[8,128,512]{2,1,0:T(8,128)S(1)} %all_to_all.25.in_ref, f32[8,4,2,64,128]{4,3,2,1,0:T(8,128)} %all-to-all-done.3.w_ref), custom_call_target="tpu_custom_call" | custom-call | flops 3600000000 | bytes 8000000 | tf_op jit(solution)/shard_map/last_levels/pallas_call | solution.py:116
  169.4 65.0 %all_to_all.26 = f32[128,64,128]{2,1,0:T(8,128)S(1)} all-to-all(f32[128,64,128]{2,1,0:T(8,128)} %bitcast.12), channel_id=1, replica_groups=mesh['gx'=8,'gy'=16] {'gx','gy'}, dimensions={0} | all-to-all | bytes 8388608 | tf_op jit(solution)/shard_map/all_to_all | solution.py:152
  234.4 4.4 %copy.6 = f32[8,8,2,4,2,8,128]{6,1,2,0,5,3,4:T(8,128)} copy(f32[8,8,2,4,2,8,128]{6,5,4,3,2,1,0:T(8,128)S(1)} %bitcast.11) | data formatting | bytes 8388608 | tf_op jit(solution)/shard_map/reshape | solution.py:153
Async XLA Ops:
  5.3 8.5 %copy-start = (f32[2,8,64,512]{3,2,1,0:T(8,128)S(1)}, f32[2,8,64,512]{3,2,1,0:T(8,128)}, u32[]{:S(2)}) copy-start(f32[2,8,64,512]{3,2,1,0:T(8,128)} %own_ref.1) | copy-start | bytes 6291460
  5.3 54.0 %all-to-all-start.1 = ((f32[8,7,2,64,128]{4,3,2,1,0:T(8,128)}), f32[8,7,2,64,128]{4,3,2,1,0:T(8,128)}, u32[]{:S(2)}, u32[]{:S(2)}) async-start(f32[8,7,2,64,128]{4,3,2,1,0:T(8,128)} %maximum_bitcast_fusion), calls=%async_computation.1 | async-start | bytes 7340032 | tf_op jit(solution)/shard_map/all_to_all | solution.py:136
  13.8 5.0 %collective-permute-start = (f32[2,8,64,512]{3,2,1,0:T(8,128)S(1)}, f32[2,8,64,512]{3,2,1,0:T(8,128)}, u32[]{:S(2)}, u32[]{:S(2)}) collective-permute-start(f32[2,8,64,512]{3,2,1,0:T(8,128)S(1)} %copy-done), channel_id=1, source_target_pairs={{0,1},{1,0},{2,3},{3,2},{4,5},{5,4},{6,7},{7,6},{8,9},{9,8},{10,11... | collective-permute-start | bytes 6291464 | tf_op jit(solution)/shard_map/ppermute | solution.py:142
  59.3 42.0 %all-to-all-start = ((f32[8,128,512]{2,1,0:T(8,128)}), f32[8,128,512]{2,1,0:T(8,128)S(1)}, u32[]{:S(2)}, u32[]{:S(2)}) async-start(f32[8,128,512]{2,1,0:T(8,128)} %first_level.1), calls=%async_computation | async-start | bytes 4194304 | tf_op jit(solution)/shard_map/all_to_all | solution.py:136
  101.3 31.6 %all-to-all-start.3 = ((f32[8,4,2,64,128]{4,3,2,1,0:T(8,128)}), f32[8,4,2,64,128]{4,3,2,1,0:T(8,128)}, u32[]{:S(2)}, u32[]{:S(2)}) async-start(f32[8,4,2,64,128]{4,3,2,1,0:T(8,128)} %slice.8), calls=%async_computation.3 | async-start | bytes 4194304 | tf_op jit(solution)/shard_map/all_to_all | solution.py:139
  110.4 1.3 copy-start.1

commit v2 on v1

v2 whole, which is shorter than its diff:
```python
import jax
import jax.numpy as jnp
from jax import lax
from jax.experimental import pallas as pl
from jax.experimental.pallas import tpu as pltpu
from jax.sharding import PartitionSpec as P

AXES = ("gx", "gy")
TILE = 256
VMEM_BYTES = 48 * 1024 * 1024
ALL_VMEM_BYTES = 60 * 1024 * 1024


def halves(value):
    high = value.astype(jnp.bfloat16)
    return high, (value - high.astype(jnp.float32)).astype(jnp.bfloat16)


def dot3(a_high, a_low, b_high, b_low):
    rows = a_high.shape[0]
    both = jnp.dot(jnp.concatenate([a_high, a_low], 0), b_high, preferred_element_type=jnp.float32)
    return both[:rows] + both[rows:] + jnp.dot(a_high, b_low, preferred_element_type=jnp.float32)


def real_rows(real, imag):
    return jnp.concatenate([jnp.concatenate([real, -imag], 1), jnp.concatenate([imag, real], 1)], 0)


def first_level_kernel(bit_ref, own_ref, other_ref, w_ref, out_ref):
    swap = bit_ref[0] == 1
    real, imag = w_ref[0, 0, 0], w_ref[0, 1, 0]
    real = jnp.where(swap, pltpu.roll(real, 64, 1), real)
    imag = jnp.where(swap, pltpu.roll(imag, 64, 1), imag)
    block = real_rows(real, imag)
    coeffs = jnp.concatenate([own_ref[0, 0], other_ref[0, 0], own_ref[1, 0], other_ref[1, 0]], 0)
    out_ref[0] = dot3(*halves(block), *halves(coeffs))


def first_level(bit, own, other, weights):
    _, boxes, rank, frames = own.shape
    state = pl.BlockSpec((2, 1, rank, frames), lambda k, bit: (0, k, 0, 0))
    return pl.pallas_call(
        first_level_kernel,
        out_shape=jax.ShapeDtypeStruct((boxes, 2 * rank, frames), jnp.float32),
        grid_spec=pltpu.PrefetchScalarGridSpec(
            num_scalar_prefetch=1,
            grid=(boxes,),
            in_specs=[
                state,
                state,
                pl.BlockSpec((1, 2, 1, rank, 2 * rank), lambda k, bit: (0, 0, k, 0, 0)),
            ],
            out_specs=pl.BlockSpec((1, 2 * rank, frames), lambda k, bit: ((k & 3) * 2 + (k >> 2), 0, 0)),
        ),
        compiler_params=pltpu.CompilerParams(vmem_limit_bytes=VMEM_BYTES),
        cost_estimate=pl.CostEstimate(flops=900_000_000, bytes_accessed=7_000_000, transcendentals=0),
        name="first_level",
    )(bit, own, other, weights)


def one_level(state_ref, w_ref, at, pairs):
    rank = state_ref.shape[1] // 2
    for (low, w_low), (high, w_high) in pairs:
        block = jnp.concatenate(
            [real_rows(w_ref[w_low, at, 0], w_ref[w_low, at, 1]), real_rows(w_ref[w_high, at, 0], w_ref[w_high, at, 1])], 0
        )
        coeffs = jnp.concatenate(
            [state_ref[low, :rank], state_ref[high, :rank], state_ref[low, rank:], state_ref[high, rank:]], 0
        )
        new = dot3(*halves(block), *halves(coeffs))
        state_ref[low] = new[: 2 * rank]
        state_ref[high] = new[2 * rank :]


def pairs_of(mask):
    return [((b, b), (b | mask, b | mask)) for b in range(8) if not b & mask]


def y_levels_kernel(in_ref, w_ref, out_ref):
    out_ref[...] = in_ref[...]
    for at, mask in enumerate((2, 4)):
        one_level(out_ref, w_ref, at, pairs_of(mask))


def y_levels(state, weights):
    boxes, rows, frames = state.shape
    tile = pl.BlockSpec((boxes, rows, TILE), lambda i: (0, 0, i))
    return pl.pallas_call(
        y_levels_kernel,
        out_shape=jax.ShapeDtypeStruct(state.shape, jnp.float32),
        grid=(frames // TILE,),
        in_specs=[tile, pl.BlockSpec(weights.shape, lambda i: (0, 0, 0, 0, 0))],
        out_specs=tile,
        compiler_params=pltpu.CompilerParams(vmem_limit_bytes=ALL_VMEM_BYTES),
        cost_estimate=pl.CostEstimate(flops=1_800_000_000, bytes_accessed=5_000_000, transcendentals=0),
        name="y_levels",
    )(state, weights)


def z_level_kernel(me_ref, in_ref, keep_ref, came_ref, out_ref, w_ref):
    w_ref[me_ref[1], 0] = keep_ref[0]
    w_ref[1 - me_ref[1], 0] = came_ref[0]
    out_ref[...] = in_ref[...]
    one_level(out_ref, w_ref, 0, [((0, 0), (1, 1))])


def z_level(me, state, keep, came):
    boxes, rows, frames = state.shape
    pair = pl.BlockSpec((2, rows, frames), lambda i, me: (i, 0, 0))
    block = pl.BlockSpec((1,) + keep.shape[1:], lambda i, me: (i, 0, 0, 0))
    return pl.pallas_call(
        z_level_kernel,
        out_shape=jax.ShapeDtypeStruct(state.shape, jnp.float32),
        grid_spec=pltpu.PrefetchScalarGridSpec(
            num_scalar_prefetch=1,
            grid=(boxes // 2,),
            in_specs=[pair, block, block],
            out_specs=pair,
            scratch_shapes=[pltpu.VMEM((2, 1) + keep.shape[1:], jnp.float32)],
        ),
        compiler_params=pltpu.CompilerParams(vmem_limit_bytes=VMEM_BYTES),
        cost_estimate=pl.CostEstimate(flops=900_000_000, bytes_accessed=4_500_000, transcendentals=0),
        name="z_level",
    )(me, state, keep, came)


def last_levels_kernel(me_ref, in_ref, *refs):
    *late_refs, out_ref, w_ref, state_ref = refs

    @pl.when(pl.program_id(0) == 0)
    def _():
        for i, late_ref in enumerate(late_refs):
            for j in range(2):
                w_ref[(me_ref[0] ^ i) * 2 + (me_ref[1] ^ j)] = late_ref[j]

    state_ref[...] = in_ref[...]
    for at, mask in enumerate((2, 4, 1)):
        one_level(state_ref, w_ref, at, pairs_of(mask))
    boxes = state_ref.shape[0]
    for box in range(boxes):
        real, imag = w_ref[box, 3, 0], w_ref[box, 3, 1]
        block = jnp.concatenate([jnp.concatenate([real, imag], 1), jnp.concatenate([-imag, real], 1)], 0)
        samples = dot3(*halves(jnp.transpose(state_ref[box])), *halves(block))
        columns = real.shape[1]
        count = samples.shape[0]
        out_ref[pl.ds(box, count, stride=2 * boxes), :] = samples[:, :columns]
        out_ref[pl.ds(boxes + box, count, stride=2 * boxes), :] = samples[:, columns:]


def last_levels(me, state, late):
    boxes, rows, frames = state.shape
    return pl.pallas_call(
        last_levels_kernel,
        out_shape=jax.ShapeDtypeStruct((frames * 2 * boxes, rows), jnp.float32),
        grid_spec=pltpu.PrefetchScalarGridSpec(
            num_scalar_prefetch=1,
            grid=(frames // TILE,),
            in_specs=[pl.BlockSpec((boxes, rows, TILE), lambda i, me: (0, 0, i))]
            + [pl.BlockSpec(late[0].shape, lambda i, me: (0, 0, 0, 0, 0))] * 4,
            out_specs=pl.BlockSpec((TILE * 2 * boxes, rows), lambda i, me: (i, 0)),
            scratch_shapes=[
                pltpu.VMEM((boxes,) + late[0].shape[1:], jnp.float32),
                pltpu.VMEM((boxes, rows, TILE), jnp.float32),
            ],
        ),
        compiler_params=pltpu.CompilerParams(vmem_limit_bytes=VMEM_BYTES),
        cost_estimate=pl.CostEstimate(flops=3_600_000_000, bytes_accessed=8_000_000, transcendentals=0),
        name="last_levels",
    )(me, state, *late)


def early_kernel(w_ref, out_ref):
    for box in range(8):
        for part in range(2):
            out_ref[(box & 3) * 2 + (box >> 2), 0, part] = w_ref[0, part, box]


def early_blocks(weights):
    _, _, boxes, rank, columns = weights.shape
    return pl.pallas_call(
        early_kernel,
        out_shape=jax.ShapeDtypeStruct((boxes, 2, 2, rank, columns), jnp.float32),
        grid=(2,),
        in_specs=[pl.BlockSpec((1, 2, boxes, rank, columns), lambda i: (i + 1, 0, 0, 0, 0))],
        out_specs=pl.BlockSpec((boxes, 1, 2, rank, columns), lambda i: (0, i, 0, 0, 0)),
        compiler_params=pltpu.CompilerParams(vmem_limit_bytes=ALL_VMEM_BYTES),
        cost_estimate=pl.CostEstimate(flops=0, bytes_accessed=2_000_000, transcendentals=0),
        name="early_blocks",
    )(weights)


def late_kernel(me_ref, w_ref, interp_ref, keep1_ref, keep2_ref, give1_ref, give2_ref, keep3_ref, give3_ref):
    step = pl.program_id(0)
    last = pl.num_programs(0) - 1
    x, z_hi = me_ref[0], me_ref[1]

    @pl.when(step == 0)
    def _():
        for low in range(4):
            for part in range(2):
                keep3_ref[low, part] = w_ref[0, part, low + 4 * z_hi]
                give3_ref[low, part] = w_ref[0, part, low + 4 * (1 - z_hi)]

    def put(block):
        for at, keep_ref, give_ref in ((0, keep1_ref, give1_ref), (2, keep2_ref, give2_ref)):
            for i in range(2):
                for part in range(2):
                    keep_ref[i, 0, part] = block(part, (x ^ (at + i)) + 4 * z_hi)
                    give_ref[i, 0, part] = block(part, (x ^ (at + i)) + 4 * (1 - z_hi))

    @pl.when((step > 0) & (step < last))
    def _():
        put(lambda part, box: w_ref[0, part, box])

    @pl.when(step == last)
    def _():
        put(lambda part, box: interp_ref[part, box])


def late_blocks(me, weights, interp):
    levels, _, boxes, rank, columns = weights.shape
    half = jax.ShapeDtypeStruct((2, 4, 2, rank, columns), jnp.float32)
    third = jax.ShapeDtypeStruct((4, 2, rank, columns), jnp.float32)
    half_spec = pl.BlockSpec((2, 1, 2, rank, columns), lambda i, me: (0, jnp.maximum(i - 1, 0), 0, 0, 0))
    third_spec = pl.BlockSpec((4, 2, rank, columns), lambda i, me: (0, 0, 0, 0))
    return pl.pallas_call(
        late_kernel,
        out_shape=[half, half, half, half, third, third],
        grid_spec=pltpu.PrefetchScalarGridSpec(
            num_scalar_prefetch=1,
            grid=(5,),
            in_specs=[
                pl.BlockSpec(
                    (1, 2, boxes, rank, columns), lambda i, me: (jnp.minimum(i + 3, levels - 1), 0, 0, 0, 0)
                ),
                pl.BlockSpec((2, boxes, rank, columns), lambda i, me: (0, 0, 0, 0)),
            ],
            out_specs=[half_spec] * 4 + [third_spec] * 2,
        ),
        compiler_params=pltpu.CompilerParams(vmem_limit_bytes=ALL_VMEM_BYTES),
        cost_estimate=pl.CostEstimate(flops=0, bytes_accessed=5_000_000, transcendentals=0),
        name="late_blocks",
    )(me, weights, interp)


def order_kernel(in_ref, out_ref):
    for z_lo in range(2):
        for low in range(8):
            first = z_lo * 64 + low
            tile = jnp.concatenate(
                [in_ref[pl.ds(first, 4, stride=16)], in_ref[pl.ds(first + 8, 4, stride=16)]], 0
            )
            tile = jnp.swapaxes(tile, 0, 1)
            for box in range(8):
                row = ((box & 1) * 4 + (box >> 1)) * 128 + z_lo * 64 + low * 8
                out_ref[0, 0, row : row + 8] = tile[box]


def in_order(samples):
    senders, rows, columns = samples.shape
    return pl.pallas_call(
        order_kernel,
        out_shape=jax.ShapeDtypeStruct((2, rows // 16, senders * 8, columns), jnp.float32),
        grid=(rows // 8,),
        in_specs=[pl.BlockSpec((senders, 8, columns), lambda i: (0, i, 0))],
        out_specs=pl.BlockSpec((1, 1, senders * 8, columns), lambda i: (i % 2, i // 2, 0, 0)),
        compiler_params=pltpu.CompilerParams(vmem_limit_bytes=VMEM_BYTES),
        cost_estimate=pl.CostEstimate(flops=0, bytes_accessed=8_000_000, transcendentals=0),
        name="in_order",
    )(samples)


def on_device(source, weights, interp):
    groups_yz = [[g * 16 + (i & 1) * 8 + (i >> 1) * 2 + c for i in range(8)] for g in range(8) for c in range(2)]
    groups_y = [[g * 16 + z * 8 + y * 2 + c for y in range(4)] for g in range(8) for z in range(2) for c in range(2)]
    groups_xz = [[((i & 1) * 4 + (i >> 1)) * 16 + h for i in range(8)] for h in range(16)]
    gx, gy = lax.axis_index("gx"), lax.axis_index("gy")
    z_lo, x, z_hi = gx >> 2, gx & 3, gy >> 3

    def swap(value, groups):
        return lax.all_to_all(value, AXES, 0, 0, axis_index_groups=groups, tiled=True)

    bit = (gy & 1).astype(jnp.int32).reshape(1)
    me = jnp.stack([x, z_hi]).astype(jnp.int32)
    other = lax.ppermute(source, "gy", [(i, i ^ 1) for i in range(16)])
    early = swap(early_blocks(weights), groups_y)

    def z_move(value, mask):
        return lax.ppermute(value, AXES, [(i, i ^ mask) for i in range(128)])

    *pieces, keep3, give3 = late_blocks(me, weights, interp)
    other, pieces = lax.optimization_barrier((other, pieces))
    came3 = z_move(give3, 8)
    at_end = z_hi == z_lo
    cames = [z_move(give, 72) for give in pieces[2:]]
    state = first_level(bit, source, other, weights)
    state, early, cames[0] = lax.optimization_barrier((state, early, cames[0]))
    stay, turned = [], []
    for keep, came in zip(pieces[:2], cames):
        stay.append(jnp.where(at_end, keep, came))
        turned.append(z_move(jnp.where(at_end, came, keep), 64))
    state = swap(state, groups_y)
    state = y_levels(state, early)
    state, came3, stay, turned = lax.optimization_barrier((state, came3, stay, turned))
    state = swap(state, groups_yz)
    late = []
    for i in range(4):
        piece = jnp.stack([stay[i // 2][i % 2], turned[i // 2][i % 2]])
        late.append(lax.ppermute(piece, "gx", [(g, g ^ i) for g in range(8)]) if i else piece)
    state = z_level(me, state, keep3, came3)
    state, *late = lax.optimization_barrier((state, *late))
    state = swap(state, groups_xz)
    samples = last_levels(me, state, late)
    samples = samples.reshape(128, -1, samples.shape[-1])
    samples = lax.all_to_all(samples, AXES, 0, 0, tiled=True)
    return in_order(samples)


def solution(mesh):
    return jax.shard_map(
        on_device,
        mesh=mesh,
        in_specs=(
            P(None, ("gx", "gy"), None, None),
            P(None, None, ("gx", "gy"), None, None),
            P(None, ("gx", "gy"), None, None),
        ),
        out_specs=P(None, ("gx", "gy"), None, None),
        check_vma=False,
    )
```

time: 240 us -> 212 us (0.88)
  waiting for transfers between devices: 84.2 us -> 44.5 us
  Pallas kernels: 19.9 us -> 34 us
  local copies, waits for them, and re-layouts: 9.99 us -> 3.55 us
  other arithmetic: 4.21 us -> 7.19 us
    all_to_all x3, waiting for transfers between devices: 80.3 us -> 25.2 us  [swap(): lax.all_to_all(value, AXES, 0, 0, axis_index_groups=groups, tiled=True)]
    ppermute x0 -> x8, waiting for transfers between devices: none -> 19.3 us  [the longest x5 17.5 us: z_move(): return lax.ppermute(value, AXES, [(i, i ^ mask) for i in range(128)])]
    all_to_all x3, starting transfers between devices: 26.4 us -> 12.5 us  [swap(): lax.all_to_all(value, AXES, 0, 0, axis_index_groups=groups, tiled=True)]
    pallas_call x1 -> x5, Pallas kernels: 4.7 us -> 18.5 us  [the longest x1 5.15 us: late_blocks(): pl.pallas_call(late_kernel, out_shape=[half, half, half, half, third, thi...]
    ppermute x0 -> x8, starting transfers between devices: none -> 13.3 us  [the longest x5 9.41 us: z_move(): return lax.ppermute(value, AXES, [(i, i ^ mask) for i in range(128)])]
    reshape x1 -> x0, local copies, waits for them, and re-layouts: 4.44 us -> none  [on_device(): samples.reshape(8, 8, 2, 4, 2, 8, 128).transpose(4, 3, 5, 0, 2, 1, 6)]
    transpose x1 -> x0, other arithmetic: 4.21 us -> none  [on_device(): jnp.concatenate([weights[1:], interp[None]], 0).transpose(2, 0, 1, 3, 4)]
    select_n x0 -> x2, other arithmetic: none -> 4 us  [on_device(): turned.append(z_move(jnp.where(at_end, came, keep), 64))]
  transfers between devices with their start and end apart: 4 -> 12, of which waited for: 4 -> 6; matrix products, arithmetic and copies ran while one was open for 1% -> 4% of each run, Pallas kernels for 5% -> 10%
where the time goes in v2:
time: 212 us; the launch traced here: 211 us
  blocking collectives  94.2 us (44%)
  waiting for transfers between devices  44.5 us (21%)
  Pallas kernels  34 us (16%)
  starting transfers between devices  27.2 us (13%)
  other arithmetic  7.19 us (3%)
  local copies, waits for them, and re-layouts  3.55 us (2%)
    all_to_all x1, blocking collectives, on_device(): samples = lax.all_to_all(samples, AXES, 0, 0, tiled=True)  68.8 us
    all_to_all x1, blocking collectives, swap(): lax.all_to_all(value, AXES, 0, 0, axis_index_groups=groups, tiled=True)  25.4 us
    all_to_all x3, waiting for transfers between devices, swap(): lax.all_to_all(value, AXES, 0, 0, axis_index_groups=groups, tiled=True)  25.2 us
    ppermute x5, waiting for transfers between devices, z_move(): return lax.ppermute(value, AXES, [(i, i ^ mask) for i in range(128)])  17.5 us
    all_to_all x3, starting transfers between devices, swap(): lax.all_to_all(value, AXES, 0, 0, axis_index_groups=groups, tiled=True)  12.5 us
    ppermute x5, starting transfers between devices, z_move(): return lax.ppermute(value, AXES, [(i, i ^ mask) for i in range(128)])  9.41 us
    pallas_call x1, Pallas kernels, last_levels(): pl.pallas_call(last_levels_kernel, out_shape=jax.ShapeDtypeStruct((frames...  8.73 us
    pallas_call x1, Pallas kernels, first_level(): pl.pallas_call(first_level_kernel, out_shape=jax.ShapeDtypeStruct((boxes,...  6.77 us
  transfers between devices with their start and end apart: 12, of which 6 were waited for; matrix products, arithmetic and copies ran while one was open for 4% of the time, Pallas kernels for 10%

profile of v2, /device:TPU:1, one launch (start us, length us, event | category | flops | bytes accessed | tf_op | source)
XLA Modules:
  0.0 210.8 jit_solution(6380521400114810022)
XLA Ops:
  0.0 1.4 collective-permute-start
  1.4 2.1 early_blocks.1
  3.5 4.3 %all-to-all-start = ((f32[8,2,2,64,128]{4,3,2,1,0:T(8,128)}), f32[8,2,2,64,128]{4,3,2,1,0:T(8,128)S(1)}, u32[]{:S(2)}, u32[]{:S(2)}) async-start(f32[8,2,2,64,128]{4,3,2,1,0:T(8,128)} %early_blocks.1), calls=%async_computation | async-start | bytes 2097152 | tf_op jit(solution)/shard_map/all_to_all | solution.py:281
  7.8 0.6 pad_add_fusion.me_ref
  8.4 0.0 copy-start
  8.4 5.2 %late_blocks.1 = (f32[2,4,2,64,128]{4,3,2,1,0:T(8,128)}, f32[2,4,2,64,128]{4,3,2,1,0:T(8,128)}, f32[2,4,2,64,128]{4,3,2,1,0:T(8,128)}, f32[2,4,2,64,128]{4,3,2,1...) custom-call(s32[2]{0:T(128)} %pad_add_fusion.me_ref, f32[7,2,8,64,128]{4,3,2,1,0:T(8,128)} %w_ref.5, ...), custom_call_target="tpu_custom_call" | custom-call | bytes 5000000 | tf_op jit(solution)/shard_map/late_blocks/pallas_call | solution.py:226
  13.5 0.0 collective-permute-done.other_ref
  13.6 3.8 %collective-permute-start.1 = (f32[2,4,2,64,128]{4,3,2,1,0:T(8,128)}, f32[2,4,2,64,128]{4,3,2,1,0:T(8,128)}, u32[]{:S(2)}, u32[]{:S(2)}) collective-permute-start(f32[2,4,2,64,128]{4,3,2,1,0:T(8,128)} %get-tuple-element.35), channel_id=1, source_target_pairs={{0,72},{1,73},{2,74},{3,75},{4,76},{5,77},{6,78},{7,79},{8,64},{9,... | collective-permute-start | bytes 1572872 | tf_op jit(solution)/shard_map/ppermute | solution.py:289
  17.4 0.0 copy-done
  17.4 6.8 %first_level.1 = f32[8,128,512]{2,1,0:T(8,128)} custom-call(s32[1]{0:T(128)} %bitcast.2.bit_ref, f32[2,8,64,512]{3,2,1,0:T(8,128)S(1)} %copy-done, f32[2,8,64,512]{3,2,1,0:T(8,128)} %collective-permute-done.other_ref, f32[7,2,8,64,128]{4,3,2,1,0:T(8,128)} %w_ref.5), custom_call_target="tpu_custom_call" | custom-call | flops 900000000 | bytes 7000000 | tf_op jit(solution)/shard_map/first_level/pallas_call | solution.py:42
  24.2 0.0 copy-start.5
  24.2 0.0 all-to-all-done.w_ref
  24.2 0.0 copy-start.4
  24.2 5.6 %collective-permute-done.1 = f32[2,4,2,64,128]{4,3,2,1,0:T(8,128)} collective-permute-done((f32[2,4,2,64,128]{4,3,2,1,0:T(8,128)}, f32[2,4,2,64,128]{4,3,2,1,0:T(8,128)}, u32[]{:S(2)}, u32[]{:S(2)}) %collective-permute-start.1) | collective-permute-done | bytes 524320 | tf_op jit(solution)/shard_map/ppermute | solution.py:289
  29.8 0.0 copy-done.4
  29.8 3.9 %all-to-all-start.1 = ((f32[8,128,512]{2,1,0:T(8,128)}), f32[8,128,512]{2,1,0:T(8,128)S(1)}, u32[]{:S(2)}, u32[]{:S(2)}) async-start(f32[8,128,512]{2,1,0:T(8,128)} %first_level.1), calls=%async_computation.1 | async-start | bytes 4194304 | tf_op jit(solution)/shard_map/all_to_all | solution.py:281
  33.7 2.4 %collective-permute-start.3 = (f32[2,4,2,64,128]{4,3,2,1,0:T(8,128)}, f32[2,4,2,64,128]{4,3,2,1,0:T(8,128)}, u32[]{:S(2)}, u32[]{:S(2)}) collective-permute-start(f32[2,4,2,64,128]{4,3,2,1,0:T(8,128)} %get-tuple-element.42), channel_id=1, source_target_pairs={{0,72},{1,73},{2,74},{3,75},{4,76},{5,77},{6,78},{7,79},{8,64},{9,... | collective-permute-start | bytes 1572872 | tf_op jit(solution)/shard_map/ppermute | solution.py:289
  36.1 0.0 copy-done.5
  36.1 1.9 broadcast_select_fusion.1
  38.0 0.0 collective-permute-start.4
  38.0 9.3 %collective-permute-done.3 = f32[2,4,2,64,128]{4,3,2,1,0:T(8,128)} collective-permute-done((f32[2,4,2,64,128]{4,3,2,1,0:T(8,128)}, f32[2,4,2,64,128]{4,3,2,1,0:T(8,128)}, u32[]{:S(2)}, u32[]{:S(2)}) %collective-permute-start.3) | collective-permute-done | bytes 524320 | tf_op jit(solution)/shard_map/ppermute | solution.py:289
  47.3 2.1 broadcast_select_fusion
  49.4 0.0 collective-permute-start.5
  49.4 3.2 %collective-permute-start.2 = (f32[4,2,64,128]{3,2,1,0:T(8,128)}, f32[4,2,64,128]{3,2,1,0:T(8,128)S(1)}, u32[]{:S(2)}, u32[]{:S(2)}) collective-permute-start(f32[4,2,64,128]{3,2,1,0:T(8,128)} %get-tuple-element.38), channel_id=1, source_target_pairs={{0,8},{1,9},{2,10},{3,11},{4,12},{5,13},{6,14},{7,15},{8,0},{9,1},... | collective-permute-start | bytes 786440 | tf_op jit(solution)/shard_map/ppermute | solution.py:289
  52.6 6.1 %all-to-all-done.1.in_ref = f32[8,128,512]{2,1,0:T(8,128)S(1)} async-done(((f32[8,128,512]{2,1,0:T(8,128)}), f32[8,128,512]{2,1,0:T(8,128)S(1)}, u32[]{:S(2)}, u32[]{:S(2)}) %all-to-all-start.1) | async-done | bytes 2097184 | tf_op jit(solution)/shard_map/all_to_all | solution.py:281
  58.7 0.0 copy-start.3
  58.7 1.3 copy-done.3
  60.0 4.8 %y_levels.1 = f32[8,128,512]{2,1,0:T(8,128)} custom-call(f32[8,128,512]{2,1,0:T(8,128)} %copy-done.3, f32[8,2,2,64,128]{4,3,2,1,0:T(8,128)} %copy-done.4), custom_call_target="tpu_custom_call" | custom-call | flops 1800000000 | bytes 5000000 | tf_op jit(solution)/shard_map/y_levels/pallas_call | solution.py:88
  64.9 2.6 %collective-permute-done.2.came_ref = f32[4,2,64,128]{3,2,1,0:T(8,128)S(1)} collective-permute-done((f32[4,2,64,128]{3,2,1,0:T(8,128)}, f32[4,2,64,128]{3,2,1,0:T(8,128)S(1)}, u32[]{:S(2)}, u32[]{:S(2)}) %collective-permute-start.2) | collective-permute-done | bytes 262176 | tf_op jit(solution)/shard_map/ppermute | solution.py:289
  67.4 0.0 collective-permute-done.4
  67.4 0.0 collective-permute-done.5
  67.4 4.4 %all-to-all-start.2 = ((f32[8,128,512]{2,1,0:T(8,128)}), f32[8,128,512]{2,1,0:T(8,128)S(1)}, u32[]{:S(2)}, u32[]{:S(2)}) async-start(f32[8,128,512]{2,1,0:T(8,128)} %y_levels.1), calls=%async_computation.2 | async-start | bytes 4194304 | tf_op jit(solution)/shard_map/all_to_all | solution.py:281
  71.8 1.1 fusion.2
  72.9 0.8 pad_maximum_fusion.1
  73.8 1.2 collective-permute-start.6
  75.0 1.1 fusion
  76.1 0.0 copy-start.1
  76.1 0.0 copy-start.2
  76.1 0.8 pad_maximum_fusion.2
  76.9 2.5 %collective-permute-start.7 = (f32[2,4,2,64,128]{4,3,2,1,0:T(8,128)}, f32[2,4,2,64,128]{4,3,2,1,0:T(8,128)}, u32[]{:S(2)}, u32[]{:S(2)}) collective-permute-start(f32[2,4,2,64,128]{4,3,2,1,0:T(8,128)} %pad_maximum_fusion.2), channel_id=1, source_target_pairs={{0,32},{16,48},{32,0},{48,16},{64,96},{80,112},{96,64},{112,80},{1... | collective-permute-start | bytes 1572872 | tf_op jit(solution)/shard_map/ppermute | solution.py:309
  79.4 0.8 pad_maximum_fusion.3
  80.2 0.2 collective-permute-start.8
  80.5 19.1 %all-to-all-done.2.in_ref = f32[8,128,512]{2,1,0:T(8,128)S(1)} async-done(((f32[8,128,512]{2,1,0:T(8,128)}), f32[8,128,512]{2,1,0:T(8,128)S(1)}, u32[]{:S(2)}, u32[]{:S(2)}) %all-to-all-start.2) | async-done | bytes 2097184 | tf_op jit(solution)/shard_map/all_to_all | solution.py:281
  99.5 0.0 copy-done.1
  99.5 0.0 copy-done.2
  99.6 2.3 %z_level.1 = f32[8,128,512]{2,1,0:T(8,128)S(1)} custom-call(s32[2]{0:T(128)S(1)} %copy-done.2, f32[8,128,512]{2,1,0:T(8,128)S(1)} %all-to-all-done.2.in_ref, f32[4,2,64,128]{3,2,1,0:T(8,128)S(1)} %copy-done.1, f32[4,2,64,128]{3,2,1,0:T(8,128)S(1)} %collective-permute-done.2.came_ref), custom_call_target="tpu_custom_call" | custom-call | flops 900000000 | bytes 4500000 | tf_op jit(solution)/shard_map/z_level/pallas_call | solution.py:111
  101.9 0.0 collective-permute-done.6.refs_1_
  101.9 0.0 collective-permute-done.7.refs_2_
  101.9 1.9 collective-permute-done.8.refs_3_
  103.8 25.4 %all_to_all.25.in_ref = f32[8,128,512]{2,1,0:T(8,128)S(1)} all-to-all(f32[8,128,512]{2,1,0:T(8,128)S(1)} %z_level.1), channel_id=1, replica_groups={{0,64,16,80,32,96,48,112},{1,65,17,81,33,97,49,113},{2,66,18,82,34,98,5..., dimensions={0} | all-to-all | bytes 4194304 | tf_op jit(solution)/shard_map/all_to_all | solution.py:281
  129.2 8.7 %last_levels.1 = f32[8192,128]{1,0:T(8,128)} custom-call(s32[2]{0:T(128)S(1)} %copy-done.2, f32[8,128,512]{2,1,0:T(8,128)S(1)} %all_to_all.25.in_ref, f32[2,4,2,64,128]{4,3,2,1,0:T(8,128)S(1)} %pad_maximum_fusion.refs_0_, f32[2,4,2,64,128]{4,3,2,1,0:T(8,128)} %collective-permute-done.6.refs_1_, f32[2,4,2,64,128]{4,3,2,1,0:T(8,128)} %collective-permute-done.7.refs_2_, ...), custom_call_target="tpu_custom_call" | custom-call | flops 3600000000 | bytes 8000000 | tf_op jit(solution)/shard_map/last_levels/pallas_call | solution.py:152
  137.9 68.8 %all_to_all.26.in_ref = f32[128,64,128]{2,1,0:T(8,128)S(1)} all-to-all(f32[128,64,128]{2,1,0:T(8,128)} %bitcast.4), channel_id=1, replica_groups=mesh['gx'=8,'gy'=16] {'gx','gy'}, dimensions={0} | all-to-all | bytes 8388608 | tf_op jit(solution)/shard_map/all_to_all | solution.py:315
  206.7 4.1 %in_order.1 = f32[2,4,1024,128]{3,2,1,0:T(8,128)} custom-call(f32[128,64,128]{2,1,0:T(8,128)S(1)} %all_to_all.26.in_ref), custom_call_target="tpu_custom_call" | custom-call | bytes 8000000 | tf_op jit(solution)/shard_map/in_order/pallas_call | solution.py:261
  (1 shorter events, 0.0 us)
Async XLA Ops:
  0.0 13.5 %collective-permute-start = (f32[2,8,64,512]{3,2,1,0:T(8,128)}, f32[2,8,64,512]{3,2,1,0:T(8,128)}, u32[]{:S(2)}, u32[]{:S(2)}) collective-permute-start(f32[2,8,64,512]{3,2,1,0:T(8,128)} %own_ref.1), channel_id=1, source_target_pairs={{0,1},{1,0},{2,3},{3,2},{4,5},{5,4},{6,7},{7,6},{8,9},{9,8},{10,11... | collective-permute-start | bytes 6291464 | tf_op jit(solution)/shard_map/ppermute | solution.py:285
  3.5 20.7 %all-to-all-start = ((f32[8,2,2,64,128]{4,3,2,1,0:T(8,128)}), f32[8,2,2,64,128]{4,3,2,1,0:T(8,128)S(1)}, u32[]{:S(2)}, u32[]{:S(2)}) async-start(f32[8,2,2,64,128]{4,3,2,1,0:T(8,128)} %early_blocks.1), calls=%async_computation | async-start | bytes 2097152 | tf_op jit(solution)/shard_map/all_to_all | solution.py:281
  8.4 9.0 %copy-start = (f32[2,8,64,512]{3,2,1,0:T(8,128)S(1)}, f32[2,8,64,512]{3,2,1,0:T(8,128)}, u32[]{:S(2)}) copy-start(f32[2,8,64,512]{3,2,1,0:T(8,128)} %own_ref.1) | copy-start | bytes 6291460
  13.6 16.2 %collective-permute-start.1 = (f32[2,4,2,64,128]{4,3,2,1,0:T(8,128)}, f32[2,4,2,64,128]{4,3,2,1,0:T(8,128)}, u32[]{:S(2)}, u32[]{:S(2)}) collective-permute-start(f32[2,4,2,64,128]{4,3,2,1,0:T(8,128)} %get-tuple-element.35), channel_id=1, source_target_pairs={{0,72},{1,73},{2,74},{3,75},{4,76},{5,77},{6,78},{7,79},{8,64},{9,... | collective-permute-start | bytes 1572872 | tf_op jit(solution)/shard_map/ppermute | solution.py:289
  24.2 11.9 %copy-start.5 = (f32[2,4,2,64,128]{4,3,2,1,0:T(8,128)S(1)}, f32[2,4,2,64,128]{4,3,2,1,0:T(8,128)}, u32[]{:S(2)}) copy-start(f32[2,4,2,64,128]{4,3,2,1,0:T(8,128)} %get-tuple-element.39) | copy-start | bytes 1572868
  24.2 5.6 %copy-start.4 = (f32[8,2,2,64,128]{4,3,2,1,0:T(8,128)}, f32[8,2,2,64,128]{4,3,2,1,0:T(8,128)S(1)}, u32[]{:S(2)}) copy-start(f32[8,2,2,64,128]{4,3,2,1,0:T(8,128)S(1)} %all-to-all-done.w_ref) | copy-start | bytes 3145732
  29.8 28.9 %all-to-all-start.1 = ((f32[8,128,512]{2,1,0:T(8,128)}), f32[8,128,512]{2,1,0:T(8,128)S(1)}, u32[]{:S(2)}, u32[]{:S(2)}) async-start(f32[8,128,512]{2,1,0:T(8,128)} %first_level.1), calls=%async_computation.1 | async-start | bytes 4194304 | tf_op jit(solution)/shard_map/all_to_all | solution.py:281
  33.7 13.6 %collective-permute-start.3 = (f32[2,4,2,64,128]{4,3,2,1,0:T(8,128)}, f32[2,4,2,64,128]{4,3,2,1,0:T(8,128)}, u32[]{:S(2)}, u32[]{:S(2)}) collective-permute-start(f32[2,4,2,64,128]{4,3,2,1,0:T(8,128)} %get-tuple-element.42), channel_id=1, source_target_pairs={{0,72},{1,73},{2,74},{3,75},{4,76},{5,77},{6,78},{7,79},{8,64},{9,... | collective-permute-start | bytes 1572872 | tf_op jit(solution)/shard_map/ppermute | solution.py:289
  38.0 29.4 %collective-permute-start.4 = (f32[2,4,2,64,128]{4,3,2,1,0:T(8,128)}, f32[2,4,2,64,128]{4,3,2,1,0:T(8,128)}, u32[]{:S(2)}, u32[]{:S(2)}) collective-permute-start(f32[2,4,2,64,128]{4,3,2,1,0:T(8,128)} %get-tuple-element.57), channel_id=1, source_target_pairs={{0,64},{1,65},{2,66},{3,67},{4,68},{5,69},{6,70},{7,71},{8,72},{9,... | collective-permute-start | bytes 1572872 | tf_op jit(solution)/shard_map/ppermute | solution.py:289
  49.4 18.1 %collective-permute-start.5 = (f32[2,4,2,64,128]{4,3,2,1,0:T(8,128)}, f32[2,4,2,64,128]{4,3,2,1,0:T(8,128)}, u32[]{:S(2)}, u32[]{:S(2)}) collective-permute-start(f32[2,4,2,64,128]{4,3,2,1,0:T(8,128)} %get-tuple-element.55), channel_id=1, source_target_pairs={{0,64},{1,65},{2,66},{3,67},{4,68},{5,69},{6,70},{7,71},{8,72},{9,... | collective-permute-start | bytes 1572872 | tf_op jit(solution)/shard_map/ppermute | solution.py:289
  49.4 18.1 %collective-permute-start.2 = (f32[4,2,64,128]{3,2,1,0:T(8,128)}, f32[4,2,64,128]{3,2,1,0:T(8,128)S(1)}, u32[]{:S(2)}, u32[]{:S(2)}) collective-permute-start(f32[4,2,64,128]{3,2,1,0:T(8,128)} %get-tuple-element.38), channel_id=1, source_target_pairs={{0,8},{1,9},{2,10},{3,11},{4,12},{5,13},{6,14},{7,15},{8,0},{9,1},... | collective-permute-start | bytes 786440 | tf_op jit(solution)/shard_map/ppermute | solution.py:289
  58.7 1.3 copy-start.3
  67.4 32.1 %all-to-all-start.2 = ((f32[8,128,512]{2,1,0:T(8,128)}), f32[8,128,512]{2,1,0:T(8,128)S(1)}, u32[]{:S(2)}, u32[]{:S(2)}) async-start(f32[8,128,512]{2,1,0:T(8,128)} %y_levels.1), calls=%async_computation.2 | async-start | bytes 4194304 | tf_op jit(solution)/shard_map/all_to_all | solution.py:281
  73.8 28.1 %collective-permute-start.6 = (f32[2,4,2,64,128]{4,3,2,1,0:T(8,128)}, f32[2,4,2,64,128]{4,3,2,1,0:T(8,128)}, u32[]{:S(2)}, u32[]{:S(2)}) collective-permute-start(f32[2,4,2,64,128]{4,3,2,1,0:T(8,128)} %pad_maximum_fusion.1), channel_id=1, source_target_pairs={{0,16},{16,0},{32,48},{48,32},{64,80},{80,64},{96,112},{112,96},{1... | collective-permute-start | bytes 1572872 | tf_op jit(solution)/shard_map/ppermute | solution.py:309
  76.1 23.5 %copy-start.1 = (f32[4,2,64,128]{3,2,1,0:T(8,128)S(1)}, f32[4,2,64,128]{3,2,1,0:T(8,128)}, u32[]{:S(2)}) copy-start(f32[4,2,64,128]{3,2,1,0:T(8,128)} %get-tuple-element.44.keep_ref) | copy-start | bytes 786436
  76.1 23.5 %copy-start.2 = (s32[2]{0:T(128)S(1)}, s32[2]{0:T(128)}, u32[]{:S(2)}) copy-start(s32[2]{0:T(128)} %pad_add_fusion.me_ref) | copy-start | bytes 28
  76.9 25.0 %collective-permute-start.7 = (f32[2,4,2,64,128]{4,3,2,1,0:T(8,128)}, f32[2,4,2,64,128]{4,3,2,1,0:T(8,128)}, u32[]{:S(2)}, u32[]{:S(2)}) collective-permute-start(f32[2,4,2,64,128]{4,3,2,1,0:T(8,128)} %pad_maximum_fusion.2), channel_id=1, source_target_pairs={{0,32},{16,48},{32,0},{48,16},{64,96},{80,112},{96,64},{112,80},{1... | collective-permute-start | bytes 1572872 | tf_op jit(solution)/shard_map/ppermute | solution.py:309
  80.2 23.5 %collective-permute-start.8 = (f32[2,4,2,64,128]{4,3,2,1,0:T(8,128)}, f32[2,4,2,64,128]{4,3,2,1,0:T(8,128)}, u32[]{:S(2)}, u32[]{:S(2)}) collective-permute-start(f32[2,4,2,64,128]{4,3,2,1,0:T(8,128)} %pad_maximum_fusion.3), channel_id=1, source_target_pairs={{0,48},{16,32},{32,16},{48,0},{64,112},{80,96},{96,80},{112,64},{1... | collective-permute-start | bytes 1572872 | tf_op jit(solution)/shard_map/ppermute | solution.py:309

commit v3 on v2

v3 whole, which is shorter than its diff:
```python
import jax
import jax.numpy as jnp
from jax import lax
from jax.experimental import pallas as pl
from jax.experimental.pallas import tpu as pltpu
from jax.sharding import PartitionSpec as P

AXES = ("gx", "gy")
TILE = 256
VMEM_BYTES = 48 * 1024 * 1024
ALL_VMEM_BYTES = 60 * 1024 * 1024


def halves(value):
    high = value.astype(jnp.bfloat16)
    return high, (value - high.astype(jnp.float32)).astype(jnp.bfloat16)


def dot3(a_high, a_low, b_high, b_low):
    left = jnp.concatenate([a_high, a_high, a_low], 1)
    right = jnp.concatenate([b_high, b_low, b_high], 0)
    return jnp.dot(left, right, preferred_element_type=jnp.float32)


def real_rows(real, imag):
    return jnp.concatenate([jnp.concatenate([real, -imag], 1), jnp.concatenate([imag, real], 1)], 0)


def first_level_kernel(bit_ref, own_ref, other_ref, w_ref, out_ref):
    swap = bit_ref[0] == 1
    for box in range(out_ref.shape[0]):
        real, imag = w_ref[0, 0, box], w_ref[0, 1, box]
        real = jnp.where(swap, pltpu.roll(real, 64, 1), real)
        imag = jnp.where(swap, pltpu.roll(imag, 64, 1), imag)
        block = real_rows(real, imag)
        coeffs = jnp.concatenate([own_ref[0, box], other_ref[0, box], own_ref[1, box], other_ref[1, box]], 0)
        out_ref[box] = dot3(*halves(block), *halves(coeffs))


def first_level(bit, own, other, weights):
    _, boxes, rank, frames = own.shape
    at_once = 2
    state = pl.BlockSpec((2, at_once, rank, frames), lambda k, bit: (0, k, 0, 0))
    return pl.pallas_call(
        first_level_kernel,
        out_shape=jax.ShapeDtypeStruct((boxes, 2 * rank, frames), jnp.float32),
        grid_spec=pltpu.PrefetchScalarGridSpec(
            num_scalar_prefetch=1,
            grid=(boxes // at_once,),
            in_specs=[
                state,
                state,
                pl.BlockSpec((1, 2, at_once, rank, 2 * rank), lambda k, bit: (0, 0, k, 0, 0)),
            ],
            out_specs=pl.BlockSpec((at_once, 2 * rank, frames), lambda k, bit: (k, 0, 0)),
        ),
        compiler_params=pltpu.CompilerParams(vmem_limit_bytes=VMEM_BYTES),
        cost_estimate=pl.CostEstimate(flops=900_000_000, bytes_accessed=7_000_000, transcendentals=0),
        name="first_level",
    )(bit, own, other, weights)


def one_level(state_ref, w_ref, at, pairs):
    rank = state_ref.shape[1] // 2
    for (low, w_low), (high, w_high) in pairs:
        block = jnp.concatenate(
            [real_rows(w_ref[w_low, at, 0], w_ref[w_low, at, 1]), real_rows(w_ref[w_high, at, 0], w_ref[w_high, at, 1])], 0
        )
        coeffs = jnp.concatenate(
            [state_ref[low, :rank], state_ref[high, :rank], state_ref[low, rank:], state_ref[high, rank:]], 0
        )
        new = dot3(*halves(block), *halves(coeffs))
        state_ref[low] = new[: 2 * rank]
        state_ref[high] = new[2 * rank :]


def pairs_of(mask):
    return [((b, b), (b | mask, b | mask)) for b in range(8) if not b & mask]


def y_levels_kernel(in_ref, w_ref, out_ref):
    out_ref[...] = in_ref[...]
    for at, mask in enumerate((2, 4)):
        one_level(out_ref, w_ref, at, pairs_of(mask))


def y_levels(state, weights):
    boxes, rows, frames = state.shape
    tile = pl.BlockSpec((boxes, rows, TILE), lambda i: (0, 0, i))
    return pl.pallas_call(
        y_levels_kernel,
        out_shape=pltpu.HBM(state.shape, jnp.float32),
        grid=(frames // TILE,),
        in_specs=[tile, pl.BlockSpec(weights.shape, lambda i: (0, 0, 0, 0, 0))],
        out_specs=tile,
        compiler_params=pltpu.CompilerParams(vmem_limit_bytes=VMEM_BYTES),
        cost_estimate=pl.CostEstimate(flops=1_800_000_000, bytes_accessed=5_000_000, transcendentals=0),
        name="y_levels",
    )(state, weights)


def z_level_kernel(mx_ref, mz_ref, in_ref, keep_ref, came_ref, out_ref, w_ref):
    w_ref[mz_ref[0], 0] = keep_ref[0]
    w_ref[1 - mz_ref[0], 0] = came_ref[0]
    out_ref[...] = in_ref[...]
    one_level(out_ref, w_ref, 0, [((0, 0), (1, 1))])


def z_level(me, state, keep, came):
    boxes, rows, frames = state.shape
    pair = pl.BlockSpec((2, rows, frames), lambda i, mx, mz: (i, 0, 0))
    block = pl.BlockSpec((1,) + keep.shape[1:], lambda i, mx, mz: (i, 0, 0, 0))
    return pl.pallas_call(
        z_level_kernel,
        out_shape=jax.ShapeDtypeStruct(state.shape, jnp.float32),
        grid_spec=pltpu.PrefetchScalarGridSpec(
            num_scalar_prefetch=2,
            grid=(boxes // 2,),
            in_specs=[pair, block, block],
            out_specs=pair,
            scratch_shapes=[pltpu.VMEM((2, 1) + keep.shape[1:], jnp.float32)],
        ),
        compiler_params=pltpu.CompilerParams(vmem_limit_bytes=VMEM_BYTES),
        cost_estimate=pl.CostEstimate(flops=900_000_000, bytes_accessed=4_500_000, transcendentals=0),
        name="z_level",
    )(*me, state, keep, came)


def last_levels_kernel(mx_ref, mz_ref, in_ref, *refs):
    *late_refs, out_ref, w_ref, state_ref = refs

    @pl.when(pl.program_id(0) == 0)
    def _():
        for i, late_ref in enumerate(late_refs):
            for j in range(2):
                w_ref[(mx_ref[0] ^ i) * 2 + (mz_ref[0] ^ j)] = late_ref[j]

    state_ref[...] = in_ref[...]
    for at, mask in enumerate((2, 4, 1)):
        one_level(state_ref, w_ref, at, pairs_of(mask))
    boxes = state_ref.shape[0]
    for box in range(boxes):
        real, imag = w_ref[box, 3, 0], w_ref[box, 3, 1]
        block = jnp.concatenate([jnp.concatenate([real, imag], 1), jnp.concatenate([-imag, real], 1)], 0)
        samples = dot3(*halves(jnp.transpose(state_ref[box])), *halves(block))
        columns = real.shape[1]
        count = samples.shape[0]
        out_ref[pl.ds(box, count, stride=2 * boxes), :] = samples[:, :columns]
        out_ref[pl.ds(boxes + box, count, stride=2 * boxes), :] = samples[:, columns:]


def last_levels(me, state, late):
    boxes, rows, frames = state.shape
    return pl.pallas_call(
        last_levels_kernel,
        out_shape=jax.ShapeDtypeStruct((frames * 2 * boxes, rows), jnp.float32),
        grid_spec=pltpu.PrefetchScalarGridSpec(
            num_scalar_prefetch=2,
            grid=(frames // TILE,),
            in_specs=[pl.BlockSpec((boxes, rows, TILE), lambda i, mx, mz: (0, 0, i))]
            + [pl.BlockSpec(late[0].shape, lambda i, mx, mz: (0, 0, 0, 0, 0))] * 4,
            out_specs=pl.BlockSpec((TILE * 2 * boxes, rows), lambda i, mx, mz: (i, 0)),
            scratch_shapes=[
                pltpu.VMEM((boxes,) + late[0].shape[1:], jnp.float32),
                pltpu.VMEM((boxes, rows, TILE), jnp.float32),
            ],
        ),
        compiler_params=pltpu.CompilerParams(vmem_limit_bytes=VMEM_BYTES),
        cost_estimate=pl.CostEstimate(flops=3_600_000_000, bytes_accessed=8_000_000, transcendentals=0),
        name="last_levels",
    )(*me, state, *late)


def pick(block_ref, part, box):
    return block_ref[(0,) * (len(block_ref.shape) - 4) + (part, box)]


def send_kernel(mx_ref, mz_ref, w1_ref, w2_ref, w4_ref, w5_ref, w6_ref, interp_ref, early_ref, *give_refs):
    for part in range(2):
        for at, block_ref in enumerate((w4_ref, w5_ref, w6_ref, interp_ref)):
            for i in range(4):
                give_refs[i // 2][i % 2, at, part] = pick(block_ref, part, (mx_ref[0] ^ i) * 2 + 1 - mz_ref[0])
        early_ref[:, 0, part] = w1_ref[0, part]
        early_ref[:, 1, part] = w2_ref[0, part]


def keep_kernel(mx_ref, mz_ref, w3_ref, w4_ref, w5_ref, w6_ref, interp_ref, keep1_ref, keep2_ref, keep3_ref, give3_ref):
    for part in range(2):
        for at, block_ref in enumerate((w4_ref, w5_ref, w6_ref, interp_ref)):
            for i in range(4):
                (keep1_ref, keep2_ref)[i // 2][i % 2, at, part] = pick(block_ref, part, (mx_ref[0] ^ i) * 2 + mz_ref[0])
        for high in range(4):
            keep3_ref[high, part] = pick(w3_ref, part, high * 2 + mz_ref[0])
            give3_ref[high, part] = pick(w3_ref, part, high * 2 + 1 - mz_ref[0])


def gather_call(kernel, name, levels, out_shapes, me, weights, interp):
    _, _, boxes, rank, columns = weights.shape

    def whole(shape):
        return pl.BlockSpec(shape, lambda i, mx, mz: (0,) * len(shape))

    def of_level(level):
        return pl.BlockSpec((1, 2, boxes, rank, columns), lambda i, mx, mz: (level, 0, 0, 0, 0))

    shapes = [shape + (2, rank, columns) for shape in out_shapes]
    return pl.pallas_call(
        kernel,
        out_shape=[jax.ShapeDtypeStruct(shape, jnp.float32) for shape in shapes],
        grid_spec=pltpu.PrefetchScalarGridSpec(
            num_scalar_prefetch=2,
            grid=(1,),
            in_specs=[of_level(level) for level in levels] + [whole(interp.shape)],
            out_specs=[whole(shape) for shape in shapes],
        ),
        compiler_params=pltpu.CompilerParams(vmem_limit_bytes=ALL_VMEM_BYTES),
        cost_estimate=pl.CostEstimate(flops=0, bytes_accessed=5_000_000, transcendentals=0),
        name=name,
    )(*me, *[weights] * len(levels), interp)


def order_kernel(in_ref, out_ref):
    for z_lo in range(2):
        for low in range(8):
            tile = jnp.swapaxes(in_ref[pl.ds(z_lo * 64 + low, 8, stride=8)], 0, 1)
            for box in range(8):
                row = ((box & 1) * 4 + (box >> 1)) * 128 + z_lo * 64 + low * 8
                out_ref[0, 0, row : row + 8] = tile[box]


def in_order(samples):
    senders, rows, columns = samples.shape
    return pl.pallas_call(
        order_kernel,
        out_shape=jax.ShapeDtypeStruct((2, rows // 16, senders * 8, columns), jnp.float32),
        grid=(rows // 8,),
        in_specs=[pl.BlockSpec((senders, 8, columns), lambda i: (0, i, 0))],
        out_specs=pl.BlockSpec((1, 1, senders * 8, columns), lambda i: (i % 2, i // 2, 0, 0)),
        compiler_params=pltpu.CompilerParams(vmem_limit_bytes=VMEM_BYTES),
        cost_estimate=pl.CostEstimate(flops=0, bytes_accessed=8_000_000, transcendentals=0),
        name="in_order",
    )(samples)


def on_device(source, weights, interp):
    groups_yz = [[g * 16 + (i & 1) * 8 + (i >> 1) * 2 + c for i in range(8)] for g in range(8) for c in range(2)]
    groups_y = [[g * 16 + z * 8 + y * 2 + c for y in range(4)] for g in range(8) for z in range(2) for c in range(2)]
    groups_xz = [[((i & 1) * 4 + (i >> 1)) * 16 + h for i in range(8)] for h in range(16)]
    gx, gy = lax.axis_index("gx"), lax.axis_index("gy")
    z_lo, x, z_hi = gx >> 2, gx & 3, gy >> 3

    def swap(value, groups):
        return lax.all_to_all(value, AXES, 0, 0, axis_index_groups=groups, tiled=True)

    bit = (gy & 1).astype(jnp.int32).reshape(1)
    me = [value.astype(jnp.int32).reshape(1) for value in (x, z_hi)]

    def z_move(value, mask):
        return lax.ppermute(value, AXES, [(i, i ^ mask) for i in range(128)])

    other = lax.ppermute(source, "gy", [(i, i ^ 1) for i in range(16)])
    early, *gives = gather_call(
        send_kernel, "send_blocks", (1, 2, 4, 5, 6), [(8, 2), (2, 4), (2, 4)], me, weights, interp
    )
    at_end = z_hi == z_lo
    cames = [z_move(give, 72) for give in gives]
    early = swap(early, groups_y)
    *keeps, keep3, give3 = gather_call(
        keep_kernel, "keep_blocks", (3, 4, 5, 6), [(2, 4), (2, 4), (4,), (4,)], me, weights, interp
    )
    other, keeps, keep3, give3 = lax.optimization_barrier((other, keeps, keep3, give3))
    came3 = z_move(give3, 8)
    state = first_level(bit, source, other, weights)
    state, early, cames[0] = lax.optimization_barrier((state, early, cames[0]))
    state = swap(state, groups_y)
    stay = [jnp.where(at_end, keep, came) for keep, came in zip(keeps, cames)]
    turned = [z_move(jnp.where(at_end, came, keep), 64) for keep, came in zip(keeps, cames)]
    state = y_levels(state, early)
    state, stay, turned = lax.optimization_barrier((state, stay, turned))
    state = swap(state, groups_yz)
    late = []
    for i in range(4):
        piece = jnp.stack([stay[i // 2][i % 2], turned[i // 2][i % 2]])
        late.append(lax.ppermute(piece, "gx", [(g, g ^ i) for g in range(8)]) if i else piece)
    state = z_level(me, state, keep3, came3)
    state, *late = lax.optimization_barrier((state, *late))
    state = swap(state, groups_xz)
    samples = last_levels(me, state, late)
    samples = samples.reshape(128, -1, samples.shape[-1])
    samples = lax.all_to_all(samples, AXES, 0, 0, tiled=True)
    return in_order(samples)


def solution(mesh):
    return jax.shard_map(
        on_device,
        mesh=mesh,
        in_specs=(
            P(None, ("gx", "gy"), None, None),
            P(None, None, ("gx", "gy"), None, None),
            P(None, ("gx", "gy"), None, None),
        ),
        out_specs=P(None, ("gx", "gy"), None, None),
        check_vma=False,
    )
```

time: 212 us -> 202 us (0.953)
  Pallas kernels: 34 us -> 27.9 us
    all_to_all x3, waiting for transfers between devices: 25.2 us -> 9.29 us  [swap(): lax.all_to_all(value, AXES, 0, 0, axis_index_groups=groups, tiled=True)]
    ppermute x5, waiting for transfers between devices: 17.5 us -> 33.3 us  [z_move(): return lax.ppermute(value, AXES, [(i, i ^ mask) for i in range(128)])]
    all_to_all x1, blocking collectives: 25.4 us -> 28.2 us  [swap(): lax.all_to_all(value, AXES, 0, 0, axis_index_groups=groups, tiled=True)]
    all_to_all x1, blocking collectives: 68.8 us -> 66 us  [on_device(): samples = lax.all_to_all(samples, AXES, 0, 0, tiled=True)]
    pallas_call x3, Pallas kernels: 12.1 us -> 9.48 us  [the longest x2 6.09 us: gather_call(): pl.pallas_call(kernel, out_shape=[jax.ShapeDtypeStruct(shape, jnp.float32...]
  transfers between devices with their start and end apart: 12 -> 12, of which waited for: 6 -> 4; matrix products, arithmetic and copies ran while one was open for 4% -> 5% of each run, Pallas kernels for 10% -> 8%
where the time goes in v3:
time: 202 us; the launch traced here: 201 us
  blocking collectives  94.3 us (47%)
  waiting for transfers between devices  42.6 us (21%)
  Pallas kernels  27.9 us (14%)
  starting transfers between devices  26.9 us (13%)
  other arithmetic  7.12 us (4%)
  local copies, waits for them, and re-layouts  2.32 us (1%)
    all_to_all x1, blocking collectives, on_device(): samples = lax.all_to_all(samples, AXES, 0, 0, tiled=True)  66 us
    ppermute x5, waiting for transfers between devices, z_move(): return lax.ppermute(value, AXES, [(i, i ^ mask) for i in range(128)])  33.3 us
    all_to_all x1, blocking collectives, swap(): lax.all_to_all(value, AXES, 0, 0, axis_index_groups=groups, tiled=True)  28.2 us
    all_to_all x3, starting transfers between devices, swap(): lax.all_to_all(value, AXES, 0, 0, axis_index_groups=groups, tiled=True)  12.5 us
    all_to_all x3, waiting for transfers between devices, swap(): lax.all_to_all(value, AXES, 0, 0, axis_index_groups=groups, tiled=True)  9.29 us
    ppermute x5, starting transfers between devices, z_move(): return lax.ppermute(value, AXES, [(i, i ^ mask) for i in range(128)])  9.07 us
    pallas_call x1, Pallas kernels, last_levels(): pl.pallas_call(last_levels_kernel, out_shape=jax.ShapeDtypeStruct((frames...  7.67 us
    pallas_call x2, Pallas kernels, gather_call(): pl.pallas_call(kernel, out_shape=[jax.ShapeDtypeStruct(shape, jnp.float32...  6.09 us
  transfers between devices with their start and end apart: 12, of which 4 were waited for; matrix products, arithmetic and copies ran while one was open for 5% of the time, Pallas kernels for 8%

profile of v3, /device:TPU:1, one launch (start us, length us, event | category | flops | bytes accessed | tf_op | source)
XLA Modules:
  0.0 201.2 jit_solution(16354814534821162516)
XLA Ops:
  0.0 1.4 collective-permute-start
  1.4 3.2 %send_blocks.1 = (f32[8,2,2,64,128]{4,3,2,1,0:T(8,128)}, f32[2,4,2,64,128]{4,3,2,1,0:T(8,128)}, f32[2,4,2,64,128]{4,3,2,1,0:T(8,128)}) custom-call(s32[1]{0:T(128)} %bitcast.mx_ref, s32[1]{0:T(128)} %bitcast.1.mz_ref, f32[7,2,8,64,128]{4,3,2,1,0:T(8,128)} %w6_ref.3, f32[7,2,8,64,128]{4,3,2,1,0:T(8,128)} %w6_ref.3, f32[7,2,8,64,128]{4,3,2,1,0:T(8,128)} %w6_ref.3, ...), custom_call_target="tpu_custom_call" | custom-call | bytes 5000000 | tf_op jit(solution)/shard_map/send_blocks/pallas_call | solution.py:207
  4.6 4.3 %all-to-all-start = ((f32[8,2,2,64,128]{4,3,2,1,0:T(8,128)}), f32[8,2,2,64,128]{4,3,2,1,0:T(8,128)S(1)}, u32[]{:S(2)}, u32[]{:S(2)}) async-start(f32[8,2,2,64,128]{4,3,2,1,0:T(8,128)} %get-tuple-element.35), calls=%async_computation | async-start | bytes 2097152 | tf_op jit(solution)/shard_map/all_to_all | solution.py:253
  8.9 0.0 copy-start
  8.9 3.8 %collective-permute-start.1 = (f32[2,4,2,64,128]{4,3,2,1,0:T(8,128)}, f32[2,4,2,64,128]{4,3,2,1,0:T(8,128)}, u32[]{:S(2)}, u32[]{:S(2)}) collective-permute-start(f32[2,4,2,64,128]{4,3,2,1,0:T(8,128)} %get-tuple-element.36), channel_id=1, source_target_pairs={{0,72},{1,73},{2,74},{3,75},{4,76},{5,77},{6,78},{7,79},{8,64},{9,... | collective-permute-start | bytes 1572872 | tf_op jit(solution)/shard_map/ppermute | solution.py:259
  12.6 2.9 %keep_blocks.1 = (f32[2,4,2,64,128]{4,3,2,1,0:T(8,128)}, f32[2,4,2,64,128]{4,3,2,1,0:T(8,128)}, f32[4,2,64,128]{3,2,1,0:T(8,128)}, f32[4,2,64,128]{3,2,1,0:T(8,128)}) custom-call(s32[1]{0:T(128)} %bitcast.mx_ref, s32[1]{0:T(128)} %bitcast.1.mz_ref, f32[7,2,8,64,128]{4,3,2,1,0:T(8,128)} %w6_ref.3, f32[7,2,8,64,128]{4,3,2,1,0:T(8,128)} %w6_ref.3, ...), custom_call_target="tpu_custom_call" | custom-call | bytes 5000000 | tf_op jit(solution)/shard_map/keep_blocks/pallas_call | solution.py:207
  15.5 0.0 collective-permute-done.other_ref
  15.5 0.0 copy-done
  15.5 4.8 %first_level.1 = f32[8,128,512]{2,1,0:T(8,128)} custom-call(s32[1]{0:T(128)} %bitcast.2.bit_ref, f32[2,8,64,512]{3,2,1,0:T(8,128)S(1)} %copy-done, f32[2,8,64,512]{3,2,1,0:T(8,128)} %collective-permute-done.other_ref, f32[7,2,8,64,128]{4,3,2,1,0:T(8,128)} %w6_ref.3), custom_call_target="tpu_custom_call" | custom-call | flops 900000000 | bytes 7000000 | tf_op jit(solution)/shard_map/first_level/pallas_call | solution.py:44
  20.3 4.7 %collective-permute-done.1 = f32[2,4,2,64,128]{4,3,2,1,0:T(8,128)} collective-permute-done((f32[2,4,2,64,128]{4,3,2,1,0:T(8,128)}, f32[2,4,2,64,128]{4,3,2,1,0:T(8,128)}, u32[]{:S(2)}, u32[]{:S(2)}) %collective-permute-start.1) | collective-permute-done | bytes 524320 | tf_op jit(solution)/shard_map/ppermute | solution.py:259
  25.0 0.0 all-to-all-done.w_ref
  25.0 3.9 %all-to-all-start.1 = ((f32[8,128,512]{2,1,0:T(8,128)}), f32[8,128,512]{2,1,0:T(8,128)S(1)}, u32[]{:S(2)}, u32[]{:S(2)}) async-start(f32[8,128,512]{2,1,0:T(8,128)} %first_level.1), calls=%async_computation.1 | async-start | bytes 4194304 | tf_op jit(solution)/shard_map/all_to_all | solution.py:253
  29.0 2.4 %collective-permute-start.2 = (f32[2,4,2,64,128]{4,3,2,1,0:T(8,128)}, f32[2,4,2,64,128]{4,3,2,1,0:T(8,128)}, u32[]{:S(2)}, u32[]{:S(2)}) collective-permute-start(f32[2,4,2,64,128]{4,3,2,1,0:T(8,128)} %get-tuple-element.42), channel_id=1, source_target_pairs={{0,72},{1,73},{2,74},{3,75},{4,76},{5,77},{6,78},{7,79},{8,64},{9,... | collective-permute-start | bytes 1572872 | tf_op jit(solution)/shard_map/ppermute | solution.py:259
  31.3 0.0 copy-start.4
  31.3 2.4 %broadcast_select_fusion.1 = (f32[2,4,2,64,128]{4,3,2,1,0:T(8,128)}, f32[2,4,2,64,128]{4,3,2,1,0:T(8,128)}) fusion(f32[2,4,2,64,128]{4,3,2,1,0:T(8,128)} %collective-permute-done.1, f32[2,4,2,64,128]{4,3,2,1,0:T(8,128)} %get-tuple-element.39, pred[]{:T(512)S(6)} %eq.3), kind=kLoop, calls=%fused_computation.5 | loop fusion | flops 262144 | bytes 2097153 | tf_op jit(solution)/shard_map/jit(_where)/select_n | solution.py:277
  33.7 0.0 collective-permute-start.3
  33.7 8.8 %collective-permute-done.2 = f32[2,4,2,64,128]{4,3,2,1,0:T(8,128)} collective-permute-done((f32[2,4,2,64,128]{4,3,2,1,0:T(8,128)}, f32[2,4,2,64,128]{4,3,2,1,0:T(8,128)}, u32[]{:S(2)}, u32[]{:S(2)}) %collective-permute-start.2) | collective-permute-done | bytes 524320 | tf_op jit(solution)/shard_map/ppermute | solution.py:259
  42.5 0.0 copy-done.4
  42.5 2.1 %broadcast_select_fusion = (f32[2,4,2,64,128]{4,3,2,1,0:T(8,128)}, f32[2,4,2,64,128]{4,3,2,1,0:T(8,128)}) fusion(f32[2,4,2,64,128]{4,3,2,1,0:T(8,128)} %collective-permute-done.2, f32[2,4,2,64,128]{4,3,2,1,0:T(8,128)S(1)} %copy-done.4, pred[]{:T(512)S(6)} %eq.3), kind=kLoop, calls=%fused_computation.4 | loop fusion | flops 262144 | bytes 2097153 | tf_op jit(solution)/shard_map/jit(_where)/select_n | solution.py:277
  44.7 0.0 collective-permute-start.4
  44.7 9.3 %all-to-all-done.1.in_ref = f32[8,128,512]{2,1,0:T(8,128)S(1)} async-done(((f32[8,128,512]{2,1,0:T(8,128)}), f32[8,128,512]{2,1,0:T(8,128)S(1)}, u32[]{:S(2)}, u32[]{:S(2)}) %all-to-all-start.1) | async-done | bytes 2097184 | tf_op jit(solution)/shard_map/all_to_all | solution.py:253
  53.9 3.4 %y_levels.1 = f32[8,128,512]{2,1,0:T(8,128)} custom-call(f32[8,128,512]{2,1,0:T(8,128)S(1)} %all-to-all-done.1.in_ref, f32[8,2,2,64,128]{4,3,2,1,0:T(8,128)S(1)} %all-to-all-done.w_ref), custom_call_target="tpu_custom_call" | custom-call | flops 1800000000 | bytes 5000000 | tf_op jit(solution)/shard_map/y_levels/pallas_call | solution.py:90
  57.3 0.0 collective-permute-done.3
  57.3 0.0 collective-permute-done.4
  57.3 0.0 copy-start.3
  57.3 4.3 %all-to-all-start.2 = ((f32[8,128,512]{2,1,0:T(8,128)}), f32[8,128,512]{2,1,0:T(8,128)S(1)}, u32[]{:S(2)}, u32[]{:S(2)}) async-start(f32[8,128,512]{2,1,0:T(8,128)} %y_levels.1), calls=%async_computation.2 | async-start | bytes 4194304 | tf_op jit(solution)/shard_map/all_to_all | solution.py:253
  61.7 0.0 copy-done.3
  61.7 0.0 copy-start.2
  61.7 1.2 fusion.2
  62.9 0.9 pad_maximum_fusion.1
  63.7 0.0 copy-start.5
  63.7 1.2 collective-permute-start.6
  65.0 0.0 copy-done.2
  65.0 1.1 fusion
  66.1 0.0 copy-start.1
  66.1 0.9 pad_maximum_fusion.2
  67.0 2.4 %collective-permute-start.7 = (f32[2,4,2,64,128]{4,3,2,1,0:T(8,128)}, f32[2,4,2,64,128]{4,3,2,1,0:T(8,128)}, u32[]{:S(2)}, u32[]{:S(2)}) collective-permute-start(f32[2,4,2,64,128]{4,3,2,1,0:T(8,128)} %pad_maximum_fusion.2), channel_id=1, source_target_pairs={{0,32},{16,48},{32,0},{48,16},{64,96},{80,112},{96,64},{112,80},{1... | collective-permute-start | bytes 1572872 | tf_op jit(solution)/shard_map/ppermute | solution.py:284
  69.4 0.8 pad_maximum_fusion.3
  70.3 0.2 collective-permute-start.8
  70.5 0.0 copy-done.5
  70.5 3.0 %collective-permute-start.5 = (f32[4,2,64,128]{3,2,1,0:T(8,128)S(1)}, f32[4,2,64,128]{3,2,1,0:T(8,128)S(1)}, u32[]{:S(2)}, u32[]{:S(2)}) collective-permute-start(f32[4,2,64,128]{3,2,1,0:T(8,128)S(1)} %copy-done.5), channel_id=1, source_target_pairs={{0,8},{1,9},{2,10},{3,11},{4,12},{5,13},{6,14},{7,15},{8,0},{9,1},... | collective-permute-start | bytes 786440 | tf_op jit(solution)/shard_map/ppermute | solution.py:259
  73.5 19.8 %collective-permute-done.5.came_ref = f32[4,2,64,128]{3,2,1,0:T(8,128)S(1)} collective-permute-done((f32[4,2,64,128]{3,2,1,0:T(8,128)S(1)}, f32[4,2,64,128]{3,2,1,0:T(8,128)S(1)}, u32[]{:S(2)}, u32[]{:S(2)}) %collective-permute-start.5) | collective-permute-done | bytes 262176 | tf_op jit(solution)/shard_map/ppermute | solution.py:259
  93.2 0.0 all-to-all-done.2.in_ref
  93.2 0.0 copy-done.1
  93.2 1.8 z_level.1
  95.0 0.0 collective-permute-done.6.refs_1_
  95.1 0.0 collective-permute-done.7.refs_2_
  95.1 0.0 collective-permute-done.8.refs_3_
  95.1 28.2 %all_to_all.25.in_ref = f32[8,128,512]{2,1,0:T(8,128)S(1)} all-to-all(f32[8,128,512]{2,1,0:T(8,128)S(1)} %z_level.1), channel_id=1, replica_groups={{0,64,16,80,32,96,48,112},{1,65,17,81,33,97,49,113},{2,66,18,82,34,98,5..., dimensions={0} | all-to-all | bytes 4194304 | tf_op jit(solution)/shard_map/all_to_all | solution.py:253
  123.3 7.7 %last_levels.1 = f32[8192,128]{1,0:T(8,128)} custom-call(s32[1]{0:T(128)} %bitcast.mx_ref, s32[1]{0:T(128)} %bitcast.1.mz_ref, f32[8,128,512]{2,1,0:T(8,128)S(1)} %all_to_all.25.in_ref, f32[2,4,2,64,128]{4,3,2,1,0:T(8,128)S(1)} %pad_maximum_fusion.refs_0_, f32[2,4,2,64,128]{4,3,2,1,0:T(8,128)} %collective-permute-done.6.refs_1_, ...), custom_call_target="tpu_custom_call" | custom-call | flops 3600000000 | bytes 8000000 | tf_op jit(solution)/shard_map/last_levels/pallas_call | solution.py:154
  131.0 66.0 %all_to_all.26.in_ref = f32[128,64,128]{2,1,0:T(8,128)S(1)} all-to-all(f32[128,64,128]{2,1,0:T(8,128)} %bitcast.4), channel_id=1, replica_groups=mesh['gx'=8,'gy'=16] {'gx','gy'}, dimensions={0} | all-to-all | bytes 8388608 | tf_op jit(solution)/shard_map/all_to_all | solution.py:290
  197.0 4.1 %in_order.1 = f32[2,4,1024,128]{3,2,1,0:T(8,128)} custom-call(f32[128,64,128]{2,1,0:T(8,128)S(1)} %all_to_all.26.in_ref), custom_call_target="tpu_custom_call" | custom-call | bytes 8000000 | tf_op jit(solution)/shard_map/in_order/pallas_call | solution.py:233
  (1 shorter events, 0.0 us)
Async XLA Ops:
  0.0 15.5 %collective-permute-start = (f32[2,8,64,512]{3,2,1,0:T(8,128)}, f32[2,8,64,512]{3,2,1,0:T(8,128)}, u32[]{:S(2)}, u32[]{:S(2)}) collective-permute-start(f32[2,8,64,512]{3,2,1,0:T(8,128)} %own_ref.1), channel_id=1, source_target_pairs={{0,1},{1,0},{2,3},{3,2},{4,5},{5,4},{6,7},{7,6},{8,9},{9,8},{10,11... | collective-permute-start | bytes 6291464 | tf_op jit(solution)/shard_map/ppermute | solution.py:261
  4.6 20.4 %all-to-all-start = ((f32[8,2,2,64,128]{4,3,2,1,0:T(8,128)}), f32[8,2,2,64,128]{4,3,2,1,0:T(8,128)S(1)}, u32[]{:S(2)}, u32[]{:S(2)}) async-start(f32[8,2,2,64,128]{4,3,2,1,0:T(8,128)} %get-tuple-element.35), calls=%async_computation | async-start | bytes 2097152 | tf_op jit(solution)/shard_map/all_to_all | solution.py:253
  8.9 6.7 %copy-start = (f32[2,8,64,512]{3,2,1,0:T(8,128)S(1)}, f32[2,8,64,512]{3,2,1,0:T(8,128)}, u32[]{:S(2)}) copy-start(f32[2,8,64,512]{3,2,1,0:T(8,128)} %own_ref.1) | copy-start | bytes 6291460
  8.9 16.2 %collective-permute-start.1 = (f32[2,4,2,64,128]{4,3,2,1,0:T(8,128)}, f32[2,4,2,64,128]{4,3,2,1,0:T(8,128)}, u32[]{:S(2)}, u32[]{:S(2)}) collective-permute-start(f32[2,4,2,64,128]{4,3,2,1,0:T(8,128)} %get-tuple-element.36), channel_id=1, source_target_pairs={{0,72},{1,73},{2,74},{3,75},{4,76},{5,77},{6,78},{7,79},{8,64},{9,... | collective-permute-start | bytes 1572872 | tf_op jit(solution)/shard_map/ppermute | solution.py:259
  25.0 28.9 %all-to-all-start.1 = ((f32[8,128,512]{2,1,0:T(8,128)}), f32[8,128,512]{2,1,0:T(8,128)S(1)}, u32[]{:S(2)}, u32[]{:S(2)}) async-start(f32[8,128,512]{2,1,0:T(8,128)} %first_level.1), calls=%async_computation.1 | async-start | bytes 4194304 | tf_op jit(solution)/shard_map/all_to_all | solution.py:253
  29.0 13.6 %collective-permute-start.2 = (f32[2,4,2,64,128]{4,3,2,1,0:T(8,128)}, f32[2,4,2,64,128]{4,3,2,1,0:T(8,128)}, u32[]{:S(2)}, u32[]{:S(2)}) collective-permute-start(f32[2,4,2,64,128]{4,3,2,1,0:T(8,128)} %get-tuple-element.42), channel_id=1, source_target_pairs={{0,72},{1,73},{2,74},{3,75},{4,76},{5,77},{6,78},{7,79},{8,64},{9,... | collective-permute-start | bytes 1572872 | tf_op jit(solution)/shard_map/ppermute | solution.py:259
  31.3 11.2 %copy-start.4 = (f32[2,4,2,64,128]{4,3,2,1,0:T(8,128)S(1)}, f32[2,4,2,64,128]{4,3,2,1,0:T(8,128)}, u32[]{:S(2)}) copy-start(f32[2,4,2,64,128]{4,3,2,1,0:T(8,128)} %get-tuple-element.41) | copy-start | bytes 1572868
  33.7 23.6 %collective-permute-start.3 = (f32[2,4,2,64,128]{4,3,2,1,0:T(8,128)}, f32[2,4,2,64,128]{4,3,2,1,0:T(8,128)}, u32[]{:S(2)}, u32[]{:S(2)}) collective-permute-start(f32[2,4,2,64,128]{4,3,2,1,0:T(8,128)} %get-tuple-element.57), channel_id=1, source_target_pairs={{0,64},{1,65},{2,66},{3,67},{4,68},{5,69},{6,70},{7,71},{8,72},{9,... | collective-permute-start | bytes 1572872 | tf_op jit(solution)/shard_map/ppermute | solution.py:259
  44.7 12.7 %collective-permute-start.4 = (f32[2,4,2,64,128]{4,3,2,1,0:T(8,128)}, f32[2,4,2,64,128]{4,3,2,1,0:T(8,128)}, u32[]{:S(2)}, u32[]{:S(2)}) collective-permute-start(f32[2,4,2,64,128]{4,3,2,1,0:T(8,128)} %get-tuple-element.55), channel_id=1, source_target_pairs={{0,64},{1,65},{2,66},{3,67},{4,68},{5,69},{6,70},{7,71},{8,72},{9,... | collective-permute-start | bytes 1572872 | tf_op jit(solution)/shard_map/ppermute | solution.py:259
  57.3 4.3 %copy-start.3 = (f32[2,4,2,64,128]{4,3,2,1,0:T(8,128)S(1)}, f32[2,4,2,64,128]{4,3,2,1,0:T(8,128)}, u32[]{:S(2)}) copy-start(f32[2,4,2,64,128]{4,3,2,1,0:T(8,128)} %get-tuple-element.46) | copy-start | bytes 1572868
  57.3 35.9 %all-to-all-start.2 = ((f32[8,128,512]{2,1,0:T(8,128)}), f32[8,128,512]{2,1,0:T(8,128)S(1)}, u32[]{:S(2)}, u32[]{:S(2)}) async-start(f32[8,128,512]{2,1,0:T(8,128)} %y_levels.1), calls=%async_computation.2 | async-start | bytes 4194304 | tf_op jit(solution)/shard_map/all_to_all | solution.py:253
  61.7 3.3 %copy-start.2 = (f32[2,4,2,64,128]{4,3,2,1,0:T(8,128)S(1)}, f32[2,4,2,64,128]{4,3,2,1,0:T(8,128)}, u32[]{:S(2)}) copy-start(f32[2,4,2,64,128]{4,3,2,1,0:T(8,128)} %get-tuple-element.48) | copy-start | bytes 1572868
  63.7 6.7 %copy-start.5 = (f32[4,2,64,128]{3,2,1,0:T(8,128)S(1)}, f32[4,2,64,128]{3,2,1,0:T(8,128)}, u32[]{:S(2)}) copy-start(f32[4,2,64,128]{3,2,1,0:T(8,128)} %get-tuple-element.45) | copy-start | bytes 786436
  63.7 31.3 %collective-permute-start.6 = (f32[2,4,2,64,128]{4,3,2,1,0:T(8,128)}, f32[2,4,2,64,128]{4,3,2,1,0:T(8,128)}, u32[]{:S(2)}, u32[]{:S(2)}) collective-permute-start(f32[2,4,2,64,128]{4,3,2,1,0:T(8,128)} %pad_maximum_fusion.1), channel_id=1, source_target_pairs={{0,16},{16,0},{32,48},{48,32},{64,80},{80,64},{96,112},{112,96},{1... | collective-permute-start | bytes 1572872 | tf_op jit(solution)/shard_map/ppermute | solution.py:284
  66.1 27.1 %copy-start.1 = (f32[4,2,64,128]{3,2,1,0:T(8,128)S(1)}, f32[4,2,64,128]{3,2,1,0:T(8,128)}, u32[]{:S(2)}) copy-start(f32[4,2,64,128]{3,2,1,0:T(8,128)} %get-tuple-element.44.keep_ref) | copy-start | bytes 786436
  67.0 28.1 %collective-permute-start.7 = (f32[2,4,2,64,128]{4,3,2,1,0:T(8,128)}, f32[2,4,2,64,128]{4,3,2,1,0:T(8,128)}, u32[]{:S(2)}, u32[]{:S(2)}) collective-permute-start(f32[2,4,2,64,128]{4,3,2,1,0:T(8,128)} %pad_maximum_fusion.2), channel_id=1, source_target_pairs={{0,32},{16,48},{32,0},{48,16},{64,96},{80,112},{96,64},{112,80},{1... | collective-permute-start | bytes 1572872 | tf_op jit(solution)/shard_map/ppermute | solution.py:284
  70.3 24.8 %collective-permute-start.8 = (f32[2,4,2,64,128]{4,3,2,1,0:T(8,128)}, f32[2,4,2,64,128]{4,3,2,1,0:T(8,128)}, u32[]{:S(2)}, u32[]{:S(2)}) collective-permute-start(f32[2,4,2,64,128]{4,3,2,1,0:T(8,128)} %pad_maximum_fusion.3), channel_id=1, source_target_pairs={{0,48},{16,32},{32,16},{48,0},{64,112},{80,96},{96,80},{112,64},{1... | collective-permute-start | bytes 1572872 | tf_op jit(solution)/shard_map/ppermute | solution.py:284
  70.5 22.8 %collective-permute-start.5 = (f32[4,2,64,128]{3,2,1,0:T(8,128)S(1)}, f32[4,2,64,128]{3,2,1,0:T(8,128)S(1)}, u32[]{:S(2)}, u32[]{:S(2)}) collective-permute-start(f32[4,2,64,128]{3,2,1,0:T(8,128)S(1)} %copy-done.5), channel_id=1, source_target_pairs={{0,8},{1,9},{2,10},{3,11},{4,12},{5,13},{6,14},{7,15},{8,0},{9,1},... | collective-permute-start | bytes 786440 | tf_op jit(solution)/shard_map/ppermute | solution.py:259

commit v4 on v3

--- a/solution.py
+++ b/solution.py
@@ -220,12 +220,14 @@
 
 
 def order_kernel(in_ref, out_ref):
-    for z_lo in range(2):
-        for low in range(8):
-            tile = jnp.swapaxes(in_ref[pl.ds(z_lo * 64 + low, 8, stride=8)], 0, 1)
-            for box in range(8):
-                row = ((box & 1) * 4 + (box >> 1)) * 128 + z_lo * 64 + low * 8
-                out_ref[0, 0, row : row + 8] = tile[box]
+    for at in range(in_ref.shape[1] // 8):
+        for z_lo in range(2):
+            for low in range(8):
+                tile = in_ref[pl.ds(z_lo * 64 + low, 8, stride=8), at * 8 : at * 8 + 8]
+                tile = jnp.swapaxes(tile, 0, 1)
+                for box in range(8):
+                    row = ((box & 1) * 4 + (box >> 1)) * 128 + z_lo * 64 + low * 8
+                    out_ref[at % 2, at // 2, row : row + 8] = tile[box]
 
 
 def in_order(samples):
@@ -233,9 +235,9 @@
     return pl.pallas_call(
         order_kernel,
         out_shape=jax.ShapeDtypeStruct((2, rows // 16, senders * 8, columns), jnp.float32),
-        grid=(rows // 8,),
-        in_specs=[pl.BlockSpec((senders, 8, columns), lambda i: (0, i, 0))],
-        out_specs=pl.BlockSpec((1, 1, senders * 8, columns), lambda i: (i % 2, i // 2, 0, 0)),
+        grid=(rows // 32,),
+        in_specs=[pl.BlockSpec((senders, 32, columns), lambda i: (0, i, 0))],
+        out_specs=pl.BlockSpec((2, 2, senders * 8, columns), lambda i: (0, i, 0, 0)),
         compiler_params=pltpu.CompilerParams(vmem_limit_bytes=VMEM_BYTES),
         cost_estimate=pl.CostEstimate(flops=0, bytes_accessed=8_000_000, transcendentals=0),
         name="in_order",

time: 202 us -> 200 us (0.990)
  no operation moved by 1% of the time
where the time goes in v4:
time: 200 us
  blocking collectives  94.3 us (47%)
  waiting for transfers between devices  42.6 us (21%)
  starting transfers between devices  26.9 us (13%)
  Pallas kernels  26.4 us (13%)
  other arithmetic  7.12 us (4%)
  local copies, waits for them, and re-layouts  2.32 us (1%)
    all_to_all x1, blocking collectives, on_device(): samples = lax.all_to_all(samples, AXES, 0, 0, tiled=True)  66 us
    ppermute x5, waiting for transfers between devices, z_move(): return lax.ppermute(value, AXES, [(i, i ^ mask) for i in range(128)])  33.3 us
    all_to_all x1, blocking collectives, swap(): lax.all_to_all(value, AXES, 0, 0, axis_index_groups=groups, tiled=True)  28.2 us
    all_to_all x3, starting transfers between devices, swap(): lax.all_to_all(value, AXES, 0, 0, axis_index_groups=groups, tiled=True)  12.5 us
    all_to_all x3, waiting for transfers between devices, swap(): lax.all_to_all(value, AXES, 0, 0, axis_index_groups=groups, tiled=True)  9.29 us
    ppermute x5, starting transfers between devices, z_move(): return lax.ppermute(value, AXES, [(i, i ^ mask) for i in range(128)])  9.07 us
    pallas_call x1, Pallas kernels, last_levels(): pl.pallas_call(last_levels_kernel, out_shape=jax.ShapeDtypeStruct((frames...  7.67 us
    pallas_call x2, Pallas kernels, gather_call(): pl.pallas_call(kernel, out_shape=[jax.ShapeDtypeStruct(shape, jnp.float32...  6.09 us
  transfers between devices with their start and end apart: 12, of which 4 were waited for; matrix products, arithmetic and copies ran while one was open for 5% of the time, Pallas kernels for 8%

profile of v4, /device:TPU:1, one launch (start us, length us, event | category | flops | bytes accessed | tf_op | source)
XLA Modules:
  0.0 199.7 jit_solution(481884425885573214)
XLA Ops:
  0.0 1.4 collective-permute-start
  1.4 3.2 %send_blocks.1 = (f32[8,2,2,64,128]{4,3,2,1,0:T(8,128)}, f32[2,4,2,64,128]{4,3,2,1,0:T(8,128)}, f32[2,4,2,64,128]{4,3,2,1,0:T(8,128)}) custom-call(s32[1]{0:T(128)} %bitcast.mx_ref, s32[1]{0:T(128)} %bitcast.1.mz_ref, f32[7,2,8,64,128]{4,3,2,1,0:T(8,128)} %w6_ref.3, f32[7,2,8,64,128]{4,3,2,1,0:T(8,128)} %w6_ref.3, f32[7,2,8,64,128]{4,3,2,1,0:T(8,128)} %w6_ref.3, ...), custom_call_target="tpu_custom_call" | custom-call | bytes 5000000 | tf_op jit(solution)/shard_map/send_blocks/pallas_call | solution.py:207
  4.6 4.3 %all-to-all-start = ((f32[8,2,2,64,128]{4,3,2,1,0:T(8,128)}), f32[8,2,2,64,128]{4,3,2,1,0:T(8,128)S(1)}, u32[]{:S(2)}, u32[]{:S(2)}) async-start(f32[8,2,2,64,128]{4,3,2,1,0:T(8,128)} %get-tuple-element.35), calls=%async_computation | async-start | bytes 2097152 | tf_op jit(solution)/shard_map/all_to_all | solution.py:255
  8.9 0.0 copy-start
  8.9 3.8 %collective-permute-start.1 = (f32[2,4,2,64,128]{4,3,2,1,0:T(8,128)}, f32[2,4,2,64,128]{4,3,2,1,0:T(8,128)}, u32[]{:S(2)}, u32[]{:S(2)}) collective-permute-start(f32[2,4,2,64,128]{4,3,2,1,0:T(8,128)} %get-tuple-element.36), channel_id=1, source_target_pairs={{0,72},{1,73},{2,74},{3,75},{4,76},{5,77},{6,78},{7,79},{8,64},{9,... | collective-permute-start | bytes 1572872 | tf_op jit(solution)/shard_map/ppermute | solution.py:261
  12.6 2.9 %keep_blocks.1 = (f32[2,4,2,64,128]{4,3,2,1,0:T(8,128)}, f32[2,4,2,64,128]{4,3,2,1,0:T(8,128)}, f32[4,2,64,128]{3,2,1,0:T(8,128)}, f32[4,2,64,128]{3,2,1,0:T(8,128)}) custom-call(s32[1]{0:T(128)} %bitcast.mx_ref, s32[1]{0:T(128)} %bitcast.1.mz_ref, f32[7,2,8,64,128]{4,3,2,1,0:T(8,128)} %w6_ref.3, f32[7,2,8,64,128]{4,3,2,1,0:T(8,128)} %w6_ref.3, ...), custom_call_target="tpu_custom_call" | custom-call | bytes 5000000 | tf_op jit(solution)/shard_map/keep_blocks/pallas_call | solution.py:207
  15.5 0.0 collective-permute-done.other_ref
  15.5 0.0 copy-done
  15.5 4.8 %first_level.1 = f32[8,128,512]{2,1,0:T(8,128)} custom-call(s32[1]{0:T(128)} %bitcast.2.bit_ref, f32[2,8,64,512]{3,2,1,0:T(8,128)S(1)} %copy-done, f32[2,8,64,512]{3,2,1,0:T(8,128)} %collective-permute-done.other_ref, f32[7,2,8,64,128]{4,3,2,1,0:T(8,128)} %w6_ref.3), custom_call_target="tpu_custom_call" | custom-call | flops 900000000 | bytes 7000000 | tf_op jit(solution)/shard_map/first_level/pallas_call | solution.py:44
  20.3 4.7 %collective-permute-done.1 = f32[2,4,2,64,128]{4,3,2,1,0:T(8,128)} collective-permute-done((f32[2,4,2,64,128]{4,3,2,1,0:T(8,128)}, f32[2,4,2,64,128]{4,3,2,1,0:T(8,128)}, u32[]{:S(2)}, u32[]{:S(2)}) %collective-permute-start.1) | collective-permute-done | bytes 524320 | tf_op jit(solution)/shard_map/ppermute | solution.py:261
  25.0 0.0 all-to-all-done.w_ref
  25.0 3.9 %all-to-all-start.1 = ((f32[8,128,512]{2,1,0:T(8,128)}), f32[8,128,512]{2,1,0:T(8,128)S(1)}, u32[]{:S(2)}, u32[]{:S(2)}) async-start(f32[8,128,512]{2,1,0:T(8,128)} %first_level.1), calls=%async_computation.1 | async-start | bytes 4194304 | tf_op jit(solution)/shard_map/all_to_all | solution.py:255
  29.0 2.4 %collective-permute-start.2 = (f32[2,4,2,64,128]{4,3,2,1,0:T(8,128)}, f32[2,4,2,64,128]{4,3,2,1,0:T(8,128)}, u32[]{:S(2)}, u32[]{:S(2)}) collective-permute-start(f32[2,4,2,64,128]{4,3,2,1,0:T(8,128)} %get-tuple-element.42), channel_id=1, source_target_pairs={{0,72},{1,73},{2,74},{3,75},{4,76},{5,77},{6,78},{7,79},{8,64},{9,... | collective-permute-start | bytes 1572872 | tf_op jit(solution)/shard_map/ppermute | solution.py:261
  31.3 0.0 copy-start.4
  31.3 2.4 %broadcast_select_fusion.1 = (f32[2,4,2,64,128]{4,3,2,1,0:T(8,128)}, f32[2,4,2,64,128]{4,3,2,1,0:T(8,128)}) fusion(f32[2,4,2,64,128]{4,3,2,1,0:T(8,128)} %collective-permute-done.1, f32[2,4,2,64,128]{4,3,2,1,0:T(8,128)} %get-tuple-element.39, pred[]{:T(512)S(6)} %eq.3), kind=kLoop, calls=%fused_computation.5 | loop fusion | flops 262144 | bytes 2097153 | tf_op jit(solution)/shard_map/jit(_where)/select_n | solution.py:279
  33.7 0.0 collective-permute-start.3
  33.7 8.8 %collective-permute-done.2 = f32[2,4,2,64,128]{4,3,2,1,0:T(8,128)} collective-permute-done((f32[2,4,2,64,128]{4,3,2,1,0:T(8,128)}, f32[2,4,2,64,128]{4,3,2,1,0:T(8,128)}, u32[]{:S(2)}, u32[]{:S(2)}) %collective-permute-start.2) | collective-permute-done | bytes 524320 | tf_op jit(solution)/shard_map/ppermute | solution.py:261
  42.5 0.0 copy-done.4
  42.5 2.1 %broadcast_select_fusion = (f32[2,4,2,64,128]{4,3,2,1,0:T(8,128)}, f32[2,4,2,64,128]{4,3,2,1,0:T(8,128)}) fusion(f32[2,4,2,64,128]{4,3,2,1,0:T(8,128)} %collective-permute-done.2, f32[2,4,2,64,128]{4,3,2,1,0:T(8,128)S(1)} %copy-done.4, pred[]{:T(512)S(6)} %eq.3), kind=kLoop, calls=%fused_computation.4 | loop fusion | flops 262144 | bytes 2097153 | tf_op jit(solution)/shard_map/jit(_where)/select_n | solution.py:279
  44.7 0.0 collective-permute-start.4
  44.7 9.3 %all-to-all-done.1.in_ref = f32[8,128,512]{2,1,0:T(8,128)S(1)} async-done(((f32[8,128,512]{2,1,0:T(8,128)}), f32[8,128,512]{2,1,0:T(8,128)S(1)}, u32[]{:S(2)}, u32[]{:S(2)}) %all-to-all-start.1) | async-done | bytes 2097184 | tf_op jit(solution)/shard_map/all_to_all | solution.py:255
  53.9 3.4 %y_levels.1 = f32[8,128,512]{2,1,0:T(8,128)} custom-call(f32[8,128,512]{2,1,0:T(8,128)S(1)} %all-to-all-done.1.in_ref, f32[8,2,2,64,128]{4,3,2,1,0:T(8,128)S(1)} %all-to-all-done.w_ref), custom_call_target="tpu_custom_call" | custom-call | flops 1800000000 | bytes 5000000 | tf_op jit(solution)/shard_map/y_levels/pallas_call | solution.py:90
  57.3 0.0 collective-permute-done.3
  57.3 0.0 collective-permute-done.4
  57.3 0.0 copy-start.3
  57.3 4.3 %all-to-all-start.2 = ((f32[8,128,512]{2,1,0:T(8,128)}), f32[8,128,512]{2,1,0:T(8,128)S(1)}, u32[]{:S(2)}, u32[]{:S(2)}) async-start(f32[8,128,512]{2,1,0:T(8,128)} %y_levels.1), calls=%async_computation.2 | async-start | bytes 4194304 | tf_op jit(solution)/shard_map/all_to_all | solution.py:255
  61.7 0.0 copy-done.3
  61.7 0.0 copy-start.2
  61.7 1.2 fusion.2
  62.9 0.9 pad_maximum_fusion.1
  63.7 0.0 copy-start.5
  63.7 1.2 collective-permute-start.6
  65.0 0.0 copy-done.2
  65.0 1.1 fusion
  66.1 0.0 copy-start.1
  66.1 0.9 pad_maximum_fusion.2
  67.0 2.4 %collective-permute-start.7 = (f32[2,4,2,64,128]{4,3,2,1,0:T(8,128)}, f32[2,4,2,64,128]{4,3,2,1,0:T(8,128)}, u32[]{:S(2)}, u32[]{:S(2)}) collective-permute-start(f32[2,4,2,64,128]{4,3,2,1,0:T(8,128)} %pad_maximum_fusion.2), channel_id=1, source_target_pairs={{0,32},{16,48},{32,0},{48,16},{64,96},{80,112},{96,64},{112,80},{1... | collective-permute-start | bytes 1572872 | tf_op jit(solution)/shard_map/ppermute | solution.py:286
  69.4 0.8 pad_maximum_fusion.3
  70.3 0.2 collective-permute-start.8
  70.5 0.0 copy-done.5
  70.5 3.0 %collective-permute-start.5 = (f32[4,2,64,128]{3,2,1,0:T(8,128)S(1)}, f32[4,2,64,128]{3,2,1,0:T(8,128)S(1)}, u32[]{:S(2)}, u32[]{:S(2)}) collective-permute-start(f32[4,2,64,128]{3,2,1,0:T(8,128)S(1)} %copy-done.5), channel_id=1, source_target_pairs={{0,8},{1,9},{2,10},{3,11},{4,12},{5,13},{6,14},{7,15},{8,0},{9,1},... | collective-permute-start | bytes 786440 | tf_op jit(solution)/shard_map/ppermute | solution.py:261
  73.5 19.8 %collective-permute-done.5.came_ref = f32[4,2,64,128]{3,2,1,0:T(8,128)S(1)} collective-permute-done((f32[4,2,64,128]{3,2,1,0:T(8,128)S(1)}, f32[4,2,64,128]{3,2,1,0:T(8,128)S(1)}, u32[]{:S(2)}, u32[]{:S(2)}) %collective-permute-start.5) | collective-permute-done | bytes 262176 | tf_op jit(solution)/shard_map/ppermute | solution.py:261
  93.2 0.0 all-to-all-done.2.in_ref
  93.2 0.0 copy-done.1
  93.2 1.8 z_level.1
  95.0 0.0 collective-permute-done.6.refs_1_
  95.1 0.0 collective-permute-done.7.refs_2_
  95.1 0.0 collective-permute-done.8.refs_3_
  95.1 28.2 %all_to_all.25.in_ref = f32[8,128,512]{2,1,0:T(8,128)S(1)} all-to-all(f32[8,128,512]{2,1,0:T(8,128)S(1)} %z_level.1), channel_id=1, replica_groups={{0,64,16,80,32,96,48,112},{1,65,17,81,33,97,49,113},{2,66,18,82,34,98,5..., dimensions={0} | all-to-all | bytes 4194304 | tf_op jit(solution)/shard_map/all_to_all | solution.py:255
  123.3 7.7 %last_levels.1 = f32[8192,128]{1,0:T(8,128)} custom-call(s32[1]{0:T(128)} %bitcast.mx_ref, s32[1]{0:T(128)} %bitcast.1.mz_ref, f32[8,128,512]{2,1,0:T(8,128)S(1)} %all_to_all.25.in_ref, f32[2,4,2,64,128]{4,3,2,1,0:T(8,128)S(1)} %pad_maximum_fusion.refs_0_, f32[2,4,2,64,128]{4,3,2,1,0:T(8,128)} %collective-permute-done.6.refs_1_, ...), custom_call_target="tpu_custom_call" | custom-call | flops 3600000000 | bytes 8000000 | tf_op jit(solution)/shard_map/last_levels/pallas_call | solution.py:154
  131.0 66.0 %all_to_all.26.in_ref = f32[128,64,128]{2,1,0:T(8,128)S(1)} all-to-all(f32[128,64,128]{2,1,0:T(8,128)} %bitcast.4), channel_id=1, replica_groups=mesh['gx'=8,'gy'=16] {'gx','gy'}, dimensions={0} | all-to-all | bytes 8388608 | tf_op jit(solution)/shard_map/all_to_all | solution.py:292
  197.0 2.7 %in_order.1 = f32[2,4,1024,128]{3,2,1,0:T(8,128)} custom-call(f32[128,64,128]{2,1,0:T(8,128)S(1)} %all_to_all.26.in_ref), custom_call_target="tpu_custom_call" | custom-call | bytes 8000000 | tf_op jit(solution)/shard_map/in_order/pallas_call | solution.py:235
  (1 shorter events, 0.0 us)
Async XLA Ops:
  0.0 15.5 %collective-permute-start = (f32[2,8,64,512]{3,2,1,0:T(8,128)}, f32[2,8,64,512]{3,2,1,0:T(8,128)}, u32[]{:S(2)}, u32[]{:S(2)}) collective-permute-start(f32[2,8,64,512]{3,2,1,0:T(8,128)} %own_ref.1), channel_id=1, source_target_pairs={{0,1},{1,0},{2,3},{3,2},{4,5},{5,4},{6,7},{7,6},{8,9},{9,8},{10,11... | collective-permute-start | bytes 6291464 | tf_op jit(solution)/shard_map/ppermute | solution.py:263
  4.6 20.4 %all-to-all-start = ((f32[8,2,2,64,128]{4,3,2,1,0:T(8,128)}), f32[8,2,2,64,128]{4,3,2,1,0:T(8,128)S(1)}, u32[]{:S(2)}, u32[]{:S(2)}) async-start(f32[8,2,2,64,128]{4,3,2,1,0:T(8,128)} %get-tuple-element.35), calls=%async_computation | async-start | bytes 2097152 | tf_op jit(solution)/shard_map/all_to_all | solution.py:255
  8.9 6.7 %copy-start = (f32[2,8,64,512]{3,2,1,0:T(8,128)S(1)}, f32[2,8,64,512]{3,2,1,0:T(8,128)}, u32[]{:S(2)}) copy-start(f32[2,8,64,512]{3,2,1,0:T(8,128)} %own_ref.1) | copy-start | bytes 6291460
  8.9 16.2 %collective-permute-start.1 = (f32[2,4,2,64,128]{4,3,2,1,0:T(8,128)}, f32[2,4,2,64,128]{4,3,2,1,0:T(8,128)}, u32[]{:S(2)}, u32[]{:S(2)}) collective-permute-start(f32[2,4,2,64,128]{4,3,2,1,0:T(8,128)} %get-tuple-element.36), channel_id=1, source_target_pairs={{0,72},{1,73},{2,74},{3,75},{4,76},{5,77},{6,78},{7,79},{8,64},{9,... | collective-permute-start | bytes 1572872 | tf_op jit(solution)/shard_map/ppermute | solution.py:261
  25.0 28.9 %all-to-all-start.1 = ((f32[8,128,512]{2,1,0:T(8,128)}), f32[8,128,512]{2,1,0:T(8,128)S(1)}, u32[]{:S(2)}, u32[]{:S(2)}) async-start(f32[8,128,512]{2,1,0:T(8,128)} %first_level.1), calls=%async_computation.1 | async-start | bytes 4194304 | tf_op jit(solution)/shard_map/all_to_all | solution.py:255
  29.0 13.6 %collective-permute-start.2 = (f32[2,4,2,64,128]{4,3,2,1,0:T(8,128)}, f32[2,4,2,64,128]{4,3,2,1,0:T(8,128)}, u32[]{:S(2)}, u32[]{:S(2)}) collective-permute-start(f32[2,4,2,64,128]{4,3,2,1,0:T(8,128)} %get-tuple-element.42), channel_id=1, source_target_pairs={{0,72},{1,73},{2,74},{3,75},{4,76},{5,77},{6,78},{7,79},{8,64},{9,... | collective-permute-start | bytes 1572872 | tf_op jit(solution)/shard_map/ppermute | solution.py:261
  31.3 11.2 %copy-start.4 = (f32[2,4,2,64,128]{4,3,2,1,0:T(8,128)S(1)}, f32[2,4,2,64,128]{4,3,2,1,0:T(8,128)}, u32[]{:S(2)}) copy-start(f32[2,4,2,64,128]{4,3,2,1,0:T(8,128)} %get-tuple-element.41) | copy-start | bytes 1572868
  33.7 23.6 %collective-permute-start.3 = (f32[2,4,2,64,128]{4,3,2,1,0:T(8,128)}, f32[2,4,2,64,128]{4,3,2,1,0:T(8,128)}, u32[]{:S(2)}, u32[]{:S(2)}) collective-permute-start(f32[2,4,2,64,128]{4,3,2,1,0:T(8,128)} %get-tuple-element.57), channel_id=1, source_target_pairs={{0,64},{1,65},{2,66},{3,67},{4,68},{5,69},{6,70},{7,71},{8,72},{9,... | collective-permute-start | bytes 1572872 | tf_op jit(solution)/shard_map/ppermute | solution.py:261
  44.7 12.7 %collective-permute-start.4 = (f32[2,4,2,64,128]{4,3,2,1,0:T(8,128)}, f32[2,4,2,64,128]{4,3,2,1,0:T(8,128)}, u32[]{:S(2)}, u32[]{:S(2)}) collective-permute-start(f32[2,4,2,64,128]{4,3,2,1,0:T(8,128)} %get-tuple-element.55), channel_id=1, source_target_pairs={{0,64},{1,65},{2,66},{3,67},{4,68},{5,69},{6,70},{7,71},{8,72},{9,... | collective-permute-start | bytes 1572872 | tf_op jit(solution)/shard_map/ppermute | solution.py:261
  57.3 4.3 %copy-start.3 = (f32[2,4,2,64,128]{4,3,2,1,0:T(8,128)S(1)}, f32[2,4,2,64,128]{4,3,2,1,0:T(8,128)}, u32[]{:S(2)}) copy-start(f32[2,4,2,64,128]{4,3,2,1,0:T(8,128)} %get-tuple-element.46) | copy-start | bytes 1572868
  57.3 35.9 %all-to-all-start.2 = ((f32[8,128,512]{2,1,0:T(8,128)}), f32[8,128,512]{2,1,0:T(8,128)S(1)}, u32[]{:S(2)}, u32[]{:S(2)}) async-start(f32[8,128,512]{2,1,0:T(8,128)} %y_levels.1), calls=%async_computation.2 | async-start | bytes 4194304 | tf_op jit(solution)/shard_map/all_to_all | solution.py:255
  61.7 3.3 %copy-start.2 = (f32[2,4,2,64,128]{4,3,2,1,0:T(8,128)S(1)}, f32[2,4,2,64,128]{4,3,2,1,0:T(8,128)}, u32[]{:S(2)}) copy-start(f32[2,4,2,64,128]{4,3,2,1,0:T(8,128)} %get-tuple-element.48) | copy-start | bytes 1572868
  63.7 6.7 %copy-start.5 = (f32[4,2,64,128]{3,2,1,0:T(8,128)S(1)}, f32[4,2,64,128]{3,2,1,0:T(8,128)}, u32[]{:S(2)}) copy-start(f32[4,2,64,128]{3,2,1,0:T(8,128)} %get-tuple-element.45) | copy-start | bytes 786436
  63.7 31.3 %collective-permute-start.6 = (f32[2,4,2,64,128]{4,3,2,1,0:T(8,128)}, f32[2,4,2,64,128]{4,3,2,1,0:T(8,128)}, u32[]{:S(2)}, u32[]{:S(2)}) collective-permute-start(f32[2,4,2,64,128]{4,3,2,1,0:T(8,128)} %pad_maximum_fusion.1), channel_id=1, source_target_pairs={{0,16},{16,0},{32,48},{48,32},{64,80},{80,64},{96,112},{112,96},{1... | collective-permute-start | bytes 1572872 | tf_op jit(solution)/shard_map/ppermute | solution.py:286
  66.1 27.1 %copy-start.1 = (f32[4,2,64,128]{3,2,1,0:T(8,128)S(1)}, f32[4,2,64,128]{3,2,1,0:T(8,128)}, u32[]{:S(2)}) copy-start(f32[4,2,64,128]{3,2,1,0:T(8,128)} %get-tuple-element.44.keep_ref) | copy-start | bytes 786436
  67.0 28.1 %collective-permute-start.7 = (f32[2,4,2,64,128]{4,3,2,1,0:T(8,128)}, f32[2,4,2,64,128]{4,3,2,1,0:T(8,128)}, u32[]{:S(2)}, u32[]{:S(2)}) collective-permute-start(f32[2,4,2,64,128]{4,3,2,1,0:T(8,128)} %pad_maximum_fusion.2), channel_id=1, source_target_pairs={{0,32},{16,48},{32,0},{48,16},{64,96},{80,112},{96,64},{112,80},{1... | collective-permute-start | bytes 1572872 | tf_op jit(solution)/shard_map/ppermute | solution.py:286
  70.3 24.8 %collective-permute-start.8 = (f32[2,4,2,64,128]{4,3,2,1,0:T(8,128)}, f32[2,4,2,64,128]{4,3,2,1,0:T(8,128)}, u32[]{:S(2)}, u32[]{:S(2)}) collective-permute-start(f32[2,4,2,64,128]{4,3,2,1,0:T(8,128)} %pad_maximum_fusion.3), channel_id=1, source_target_pairs={{0,48},{16,32},{32,16},{48,0},{64,112},{80,96},{96,80},{112,64},{1... | collective-permute-start | bytes 1572872 | tf_op jit(solution)/shard_map/ppermute | solution.py:286
  70.5 22.8 %collective-permute-start.5 = (f32[4,2,64,128]{3,2,1,0:T(8,128)S(1)}, f32[4,2,64,128]{3,2,1,0:T(8,128)S(1)}, u32[]{:S(2)}, u32[]{:S(2)}) collective-permute-start(f32[4,2,64,128]{3,2,1,0:T(8,128)S(1)} %copy-done.5), channel_id=1, source_target_pairs={{0,8},{1,9},{2,10},{3,11},{4,12},{5,13},{6,14},{7,15},{8,0},{9,1},... | collective-permute-start | bytes 786440 | tf_op jit(solution)/shard_map/ppermute | solution.py:261

commit v5 on v4

--- a/solution.py
+++ b/solution.py
@@ -86,11 +86,11 @@
 
 def y_levels(state, weights):
     boxes, rows, frames = state.shape
-    tile = pl.BlockSpec((boxes, rows, TILE), lambda i: (0, 0, i))
+    tile = pl.BlockSpec((boxes, rows, frames), lambda i: (0, 0, i))
     return pl.pallas_call(
         y_levels_kernel,
         out_shape=pltpu.HBM(state.shape, jnp.float32),
-        grid=(frames // TILE,),
+        grid=(frames // frames,),
         in_specs=[tile, pl.BlockSpec(weights.shape, lambda i: (0, 0, 0, 0, 0))],
         out_specs=tile,
         compiler_params=pltpu.CompilerParams(vmem_limit_bytes=VMEM_BYTES),
@@ -100,25 +100,27 @@
 
 
 def z_level_kernel(mx_ref, mz_ref, in_ref, keep_ref, came_ref, out_ref, w_ref):
-    w_ref[mz_ref[0], 0] = keep_ref[0]
-    w_ref[1 - mz_ref[0], 0] = came_ref[0]
+    count = keep_ref.shape[0]
+    for high in range(count):
+        w_ref[high * 2 + mz_ref[0], 0] = keep_ref[high]
+        w_ref[high * 2 + 1 - mz_ref[0], 0] = came_ref[high]
     out_ref[...] = in_ref[...]
-    one_level(out_ref, w_ref, 0, [((0, 0), (1, 1))])
+    one_level(out_ref, w_ref, 0, [((b, b), (b + 1, b + 1)) for b in range(0, 2 * count, 2)])
 
 
 def z_level(me, state, keep, came):
     boxes, rows, frames = state.shape
-    pair = pl.BlockSpec((2, rows, frames), lambda i, mx, mz: (i, 0, 0))
-    block = pl.BlockSpec((1,) + keep.shape[1:], lambda i, mx, mz: (i, 0, 0, 0))
+    pair = pl.BlockSpec((4, rows, frames), lambda i, mx, mz: (i, 0, 0))
+    block = pl.BlockSpec((2,) + keep.shape[1:], lambda i, mx, mz: (i, 0, 0, 0))
     return pl.pallas_call(
         z_level_kernel,
         out_shape=jax.ShapeDtypeStruct(state.shape, jnp.float32),
         grid_spec=pltpu.PrefetchScalarGridSpec(
             num_scalar_prefetch=2,
-            grid=(boxes // 2,),
+            grid=(boxes // 4,),
             in_specs=[pair, block, block],
             out_specs=pair,
-            scratch_shapes=[pltpu.VMEM((2, 1) + keep.shape[1:], jnp.float32)],
+            scratch_shapes=[pltpu.VMEM((4, 1) + keep.shape[1:], jnp.float32)],
         ),
         compiler_params=pltpu.CompilerParams(vmem_limit_bytes=VMEM_BYTES),
         cost_estimate=pl.CostEstimate(flops=900_000_000, bytes_accessed=4_500_000, transcendentals=0),

time: 200 us -> 200 us (level)
  no operation moved by 1% of the time
where the time goes in v5:
time: 200 us; the launch traced here: 199 us
  blocking collectives  94.2 us (47%)
  waiting for transfers between devices  42.6 us (21%)
  starting transfers between devices  26.9 us (13%)
  Pallas kernels  26.1 us (13%)
  other arithmetic  7.12 us (4%)
  local copies, waits for them, and re-layouts  2.32 us (1%)
    all_to_all x1, blocking collectives, on_device(): samples = lax.all_to_all(samples, AXES, 0, 0, tiled=True)  65.8 us
    ppermute x5, waiting for transfers between devices, z_move(): return lax.ppermute(value, AXES, [(i, i ^ mask) for i in range(128)])  33.3 us
    all_to_all x1, blocking collectives, swap(): lax.all_to_all(value, AXES, 0, 0, axis_index_groups=groups, tiled=True)  28.4 us
    all_to_all x3, starting transfers between devices, swap(): lax.all_to_all(value, AXES, 0, 0, axis_index_groups=groups, tiled=True)  12.5 us
    all_to_all x3, waiting for transfers between devices, swap(): lax.all_to_all(value, AXES, 0, 0, axis_index_groups=groups, tiled=True)  9.29 us
    ppermute x5, starting transfers between devices, z_move(): return lax.ppermute(value, AXES, [(i, i ^ mask) for i in range(128)])  9.07 us
    pallas_call x1, Pallas kernels, last_levels(): pl.pallas_call(last_levels_kernel, out_shape=jax.ShapeDtypeStruct((frames...  7.67 us
    pallas_call x2, Pallas kernels, gather_call(): pl.pallas_call(kernel, out_shape=[jax.ShapeDtypeStruct(shape, jnp.float32...  6.09 us
  transfers between devices with their start and end apart: 12, of which 4 were waited for; matrix products, arithmetic and copies ran while one was open for 5% of the time, Pallas kernels for 8%

profile of v5, /device:TPU:1, one launch (start us, length us, event | category | flops | bytes accessed | tf_op | source)
XLA Modules:
  0.0 199.4 jit_solution(3999232054572274273)
XLA Ops:
  0.0 1.4 collective-permute-start
  1.4 3.2 %send_blocks.1 = (f32[8,2,2,64,128]{4,3,2,1,0:T(8,128)}, f32[2,4,2,64,128]{4,3,2,1,0:T(8,128)}, f32[2,4,2,64,128]{4,3,2,1,0:T(8,128)}) custom-call(s32[1]{0:T(128)} %bitcast.mx_ref, s32[1]{0:T(128)} %bitcast.1.mz_ref, f32[7,2,8,64,128]{4,3,2,1,0:T(8,128)} %w6_ref.3, f32[7,2,8,64,128]{4,3,2,1,0:T(8,128)} %w6_ref.3, f32[7,2,8,64,128]{4,3,2,1,0:T(8,128)} %w6_ref.3, ...), custom_call_target="tpu_custom_call" | custom-call | bytes 5000000 | tf_op jit(solution)/shard_map/send_blocks/pallas_call | solution.py:209
  4.6 4.3 %all-to-all-start = ((f32[8,2,2,64,128]{4,3,2,1,0:T(8,128)}), f32[8,2,2,64,128]{4,3,2,1,0:T(8,128)S(1)}, u32[]{:S(2)}, u32[]{:S(2)}) async-start(f32[8,2,2,64,128]{4,3,2,1,0:T(8,128)} %get-tuple-element.35), calls=%async_computation | async-start | bytes 2097152 | tf_op jit(solution)/shard_map/all_to_all | solution.py:257
  8.9 0.0 copy-start
  8.9 3.8 %collective-permute-start.1 = (f32[2,4,2,64,128]{4,3,2,1,0:T(8,128)}, f32[2,4,2,64,128]{4,3,2,1,0:T(8,128)}, u32[]{:S(2)}, u32[]{:S(2)}) collective-permute-start(f32[2,4,2,64,128]{4,3,2,1,0:T(8,128)} %get-tuple-element.36), channel_id=1, source_target_pairs={{0,72},{1,73},{2,74},{3,75},{4,76},{5,77},{6,78},{7,79},{8,64},{9,... | collective-permute-start | bytes 1572872 | tf_op jit(solution)/shard_map/ppermute | solution.py:263
  12.6 2.9 %keep_blocks.1 = (f32[2,4,2,64,128]{4,3,2,1,0:T(8,128)}, f32[2,4,2,64,128]{4,3,2,1,0:T(8,128)}, f32[4,2,64,128]{3,2,1,0:T(8,128)}, f32[4,2,64,128]{3,2,1,0:T(8,128)}) custom-call(s32[1]{0:T(128)} %bitcast.mx_ref, s32[1]{0:T(128)} %bitcast.1.mz_ref, f32[7,2,8,64,128]{4,3,2,1,0:T(8,128)} %w6_ref.3, f32[7,2,8,64,128]{4,3,2,1,0:T(8,128)} %w6_ref.3, ...), custom_call_target="tpu_custom_call" | custom-call | bytes 5000000 | tf_op jit(solution)/shard_map/keep_blocks/pallas_call | solution.py:209
  15.5 0.0 collective-permute-done.other_ref
  15.5 0.0 copy-done
  15.5 4.8 %first_level.1 = f32[8,128,512]{2,1,0:T(8,128)} custom-call(s32[1]{0:T(128)} %bitcast.2.bit_ref, f32[2,8,64,512]{3,2,1,0:T(8,128)S(1)} %copy-done, f32[2,8,64,512]{3,2,1,0:T(8,128)} %collective-permute-done.other_ref, f32[7,2,8,64,128]{4,3,2,1,0:T(8,128)} %w6_ref.3), custom_call_target="tpu_custom_call" | custom-call | flops 900000000 | bytes 7000000 | tf_op jit(solution)/shard_map/first_level/pallas_call | solution.py:44
  20.3 4.7 %collective-permute-done.1 = f32[2,4,2,64,128]{4,3,2,1,0:T(8,128)} collective-permute-done((f32[2,4,2,64,128]{4,3,2,1,0:T(8,128)}, f32[2,4,2,64,128]{4,3,2,1,0:T(8,128)}, u32[]{:S(2)}, u32[]{:S(2)}) %collective-permute-start.1) | collective-permute-done | bytes 524320 | tf_op jit(solution)/shard_map/ppermute | solution.py:263
  25.0 0.0 all-to-all-done.w_ref
  25.0 3.9 %all-to-all-start.1 = ((f32[8,128,512]{2,1,0:T(8,128)}), f32[8,128,512]{2,1,0:T(8,128)S(1)}, u32[]{:S(2)}, u32[]{:S(2)}) async-start(f32[8,128,512]{2,1,0:T(8,128)} %first_level.1), calls=%async_computation.1 | async-start | bytes 4194304 | tf_op jit(solution)/shard_map/all_to_all | solution.py:257
  29.0 2.4 %collective-permute-start.2 = (f32[2,4,2,64,128]{4,3,2,1,0:T(8,128)}, f32[2,4,2,64,128]{4,3,2,1,0:T(8,128)}, u32[]{:S(2)}, u32[]{:S(2)}) collective-permute-start(f32[2,4,2,64,128]{4,3,2,1,0:T(8,128)} %get-tuple-element.42), channel_id=1, source_target_pairs={{0,72},{1,73},{2,74},{3,75},{4,76},{5,77},{6,78},{7,79},{8,64},{9,... | collective-permute-start | bytes 1572872 | tf_op jit(solution)/shard_map/ppermute | solution.py:263
  31.3 0.0 copy-start.4
  31.3 2.4 %broadcast_select_fusion.1 = (f32[2,4,2,64,128]{4,3,2,1,0:T(8,128)}, f32[2,4,2,64,128]{4,3,2,1,0:T(8,128)}) fusion(f32[2,4,2,64,128]{4,3,2,1,0:T(8,128)} %collective-permute-done.1, f32[2,4,2,64,128]{4,3,2,1,0:T(8,128)} %get-tuple-element.39, pred[]{:T(512)S(6)} %eq.3), kind=kLoop, calls=%fused_computation.5 | loop fusion | flops 262144 | bytes 2097153 | tf_op jit(solution)/shard_map/jit(_where)/select_n | solution.py:281
  33.7 0.0 collective-permute-start.3
  33.7 8.8 %collective-permute-done.2 = f32[2,4,2,64,128]{4,3,2,1,0:T(8,128)} collective-permute-done((f32[2,4,2,64,128]{4,3,2,1,0:T(8,128)}, f32[2,4,2,64,128]{4,3,2,1,0:T(8,128)}, u32[]{:S(2)}, u32[]{:S(2)}) %collective-permute-start.2) | collective-permute-done | bytes 524320 | tf_op jit(solution)/shard_map/ppermute | solution.py:263
  42.5 0.0 copy-done.4
  42.5 2.1 %broadcast_select_fusion = (f32[2,4,2,64,128]{4,3,2,1,0:T(8,128)}, f32[2,4,2,64,128]{4,3,2,1,0:T(8,128)}) fusion(f32[2,4,2,64,128]{4,3,2,1,0:T(8,128)} %collective-permute-done.2, f32[2,4,2,64,128]{4,3,2,1,0:T(8,128)S(1)} %copy-done.4, pred[]{:T(512)S(6)} %eq.3), kind=kLoop, calls=%fused_computation.4 | loop fusion | flops 262144 | bytes 2097153 | tf_op jit(solution)/shard_map/jit(_where)/select_n | solution.py:281
  44.7 0.0 collective-permute-start.4
  44.7 9.3 %all-to-all-done.1.in_ref = f32[8,128,512]{2,1,0:T(8,128)S(1)} async-done(((f32[8,128,512]{2,1,0:T(8,128)}), f32[8,128,512]{2,1,0:T(8,128)S(1)}, u32[]{:S(2)}, u32[]{:S(2)}) %all-to-all-start.1) | async-done | bytes 2097184 | tf_op jit(solution)/shard_map/all_to_all | solution.py:257
  53.9 3.2 %y_levels.1 = f32[8,128,512]{2,1,0:T(8,128)} custom-call(f32[8,128,512]{2,1,0:T(8,128)S(1)} %all-to-all-done.1.in_ref, f32[8,2,2,64,128]{4,3,2,1,0:T(8,128)S(1)} %all-to-all-done.w_ref), custom_call_target="tpu_custom_call" | custom-call | flops 1800000000 | bytes 5000000 | tf_op jit(solution)/shard_map/y_levels/pallas_call | solution.py:90
  57.1 0.0 collective-permute-done.3
  57.1 0.0 collective-permute-done.4
  57.1 0.0 copy-start.3
  57.1 4.3 %all-to-all-start.2 = ((f32[8,128,512]{2,1,0:T(8,128)}), f32[8,128,512]{2,1,0:T(8,128)S(1)}, u32[]{:S(2)}, u32[]{:S(2)}) async-start(f32[8,128,512]{2,1,0:T(8,128)} %y_levels.1), calls=%async_computation.2 | async-start | bytes 4194304 | tf_op jit(solution)/shard_map/all_to_all | solution.py:257
  61.5 0.0 copy-done.3
  61.5 0.0 copy-start.2
  61.5 1.2 fusion.2
  62.7 0.9 pad_maximum_fusion.1
  63.5 0.0 copy-start.5
  63.5 1.2 collective-permute-start.6
  64.7 0.0 copy-done.2
  64.7 1.1 fusion
  65.9 0.0 copy-start.1
  65.9 0.9 pad_maximum_fusion.2
  66.7 2.5 %collective-permute-start.7 = (f32[2,4,2,64,128]{4,3,2,1,0:T(8,128)}, f32[2,4,2,64,128]{4,3,2,1,0:T(8,128)}, u32[]{:S(2)}, u32[]{:S(2)}) collective-permute-start(f32[2,4,2,64,128]{4,3,2,1,0:T(8,128)} %pad_maximum_fusion.2), channel_id=1, source_target_pairs={{0,32},{16,48},{32,0},{48,16},{64,96},{80,112},{96,64},{112,80},{1... | collective-permute-start | bytes 1572872 | tf_op jit(solution)/shard_map/ppermute | solution.py:288
  69.2 0.8 pad_maximum_fusion.3
  70.0 0.2 collective-permute-start.8
  70.2 0.0 copy-done.5
  70.2 3.0 %collective-permute-start.5 = (f32[4,2,64,128]{3,2,1,0:T(8,128)S(1)}, f32[4,2,64,128]{3,2,1,0:T(8,128)S(1)}, u32[]{:S(2)}, u32[]{:S(2)}) collective-permute-start(f32[4,2,64,128]{3,2,1,0:T(8,128)S(1)} %copy-done.5), channel_id=1, source_target_pairs={{0,8},{1,9},{2,10},{3,11},{4,12},{5,13},{6,14},{7,15},{8,0},{9,1},... | collective-permute-start | bytes 786440 | tf_op jit(solution)/shard_map/ppermute | solution.py:263
  73.2 19.8 %collective-permute-done.5.came_ref = f32[4,2,64,128]{3,2,1,0:T(8,128)S(1)} collective-permute-done((f32[4,2,64,128]{3,2,1,0:T(8,128)S(1)}, f32[4,2,64,128]{3,2,1,0:T(8,128)S(1)}, u32[]{:S(2)}, u32[]{:S(2)}) %collective-permute-start.5) | collective-permute-done | bytes 262176 | tf_op jit(solution)/shard_map/ppermute | solution.py:263
  93.0 0.0 all-to-all-done.2.in_ref
  93.0 0.0 copy-done.1
  93.0 1.7 z_level.1
  94.7 0.0 collective-permute-done.6.refs_1_
  94.7 0.0 collective-permute-done.7.refs_2_
  94.8 0.0 collective-permute-done.8.refs_3_
  94.8 28.4 %all_to_all.25.in_ref = f32[8,128,512]{2,1,0:T(8,128)S(1)} all-to-all(f32[8,128,512]{2,1,0:T(8,128)S(1)} %z_level.1), channel_id=1, replica_groups={{0,64,16,80,32,96,48,112},{1,65,17,81,33,97,49,113},{2,66,18,82,34,98,5..., dimensions={0} | all-to-all | bytes 4194304 | tf_op jit(solution)/shard_map/all_to_all | solution.py:257
  123.2 7.7 %last_levels.1 = f32[8192,128]{1,0:T(8,128)} custom-call(s32[1]{0:T(128)} %bitcast.mx_ref, s32[1]{0:T(128)} %bitcast.1.mz_ref, f32[8,128,512]{2,1,0:T(8,128)S(1)} %all_to_all.25.in_ref, f32[2,4,2,64,128]{4,3,2,1,0:T(8,128)S(1)} %pad_maximum_fusion.refs_0_, f32[2,4,2,64,128]{4,3,2,1,0:T(8,128)} %collective-permute-done.6.refs_1_, ...), custom_call_target="tpu_custom_call" | custom-call | flops 3600000000 | bytes 8000000 | tf_op jit(solution)/shard_map/last_levels/pallas_call | solution.py:156
  130.8 65.8 %all_to_all.26.in_ref = f32[128,64,128]{2,1,0:T(8,128)S(1)} all-to-all(f32[128,64,128]{2,1,0:T(8,128)} %bitcast.4), channel_id=1, replica_groups=mesh['gx'=8,'gy'=16] {'gx','gy'}, dimensions={0} | all-to-all | bytes 8388608 | tf_op jit(solution)/shard_map/all_to_all | solution.py:294
  196.7 2.7 %in_order.1 = f32[2,4,1024,128]{3,2,1,0:T(8,128)} custom-call(f32[128,64,128]{2,1,0:T(8,128)S(1)} %all_to_all.26.in_ref), custom_call_target="tpu_custom_call" | custom-call | bytes 8000000 | tf_op jit(solution)/shard_map/in_order/pallas_call | solution.py:237
  (1 shorter events, 0.0 us)
Async XLA Ops:
  0.0 15.5 %collective-permute-start = (f32[2,8,64,512]{3,2,1,0:T(8,128)}, f32[2,8,64,512]{3,2,1,0:T(8,128)}, u32[]{:S(2)}, u32[]{:S(2)}) collective-permute-start(f32[2,8,64,512]{3,2,1,0:T(8,128)} %own_ref.1), channel_id=1, source_target_pairs={{0,1},{1,0},{2,3},{3,2},{4,5},{5,4},{6,7},{7,6},{8,9},{9,8},{10,11... | collective-permute-start | bytes 6291464 | tf_op jit(solution)/shard_map/ppermute | solution.py:265
  4.6 20.4 %all-to-all-start = ((f32[8,2,2,64,128]{4,3,2,1,0:T(8,128)}), f32[8,2,2,64,128]{4,3,2,1,0:T(8,128)S(1)}, u32[]{:S(2)}, u32[]{:S(2)}) async-start(f32[8,2,2,64,128]{4,3,2,1,0:T(8,128)} %get-tuple-element.35), calls=%async_computation | async-start | bytes 2097152 | tf_op jit(solution)/shard_map/all_to_all | solution.py:257
  8.9 6.7 %copy-start = (f32[2,8,64,512]{3,2,1,0:T(8,128)S(1)}, f32[2,8,64,512]{3,2,1,0:T(8,128)}, u32[]{:S(2)}) copy-start(f32[2,8,64,512]{3,2,1,0:T(8,128)} %own_ref.1) | copy-start | bytes 6291460
  8.9 16.2 %collective-permute-start.1 = (f32[2,4,2,64,128]{4,3,2,1,0:T(8,128)}, f32[2,4,2,64,128]{4,3,2,1,0:T(8,128)}, u32[]{:S(2)}, u32[]{:S(2)}) collective-permute-start(f32[2,4,2,64,128]{4,3,2,1,0:T(8,128)} %get-tuple-element.36), channel_id=1, source_target_pairs={{0,72},{1,73},{2,74},{3,75},{4,76},{5,77},{6,78},{7,79},{8,64},{9,... | collective-permute-start | bytes 1572872 | tf_op jit(solution)/shard_map/ppermute | solution.py:263
  25.0 28.9 %all-to-all-start.1 = ((f32[8,128,512]{2,1,0:T(8,128)}), f32[8,128,512]{2,1,0:T(8,128)S(1)}, u32[]{:S(2)}, u32[]{:S(2)}) async-start(f32[8,128,512]{2,1,0:T(8,128)} %first_level.1), calls=%async_computation.1 | async-start | bytes 4194304 | tf_op jit(solution)/shard_map/all_to_all | solution.py:257
  29.0 13.6 %collective-permute-start.2 = (f32[2,4,2,64,128]{4,3,2,1,0:T(8,128)}, f32[2,4,2,64,128]{4,3,2,1,0:T(8,128)}, u32[]{:S(2)}, u32[]{:S(2)}) collective-permute-start(f32[2,4,2,64,128]{4,3,2,1,0:T(8,128)} %get-tuple-element.42), channel_id=1, source_target_pairs={{0,72},{1,73},{2,74},{3,75},{4,76},{5,77},{6,78},{7,79},{8,64},{9,... | collective-permute-start | bytes 1572872 | tf_op jit(solution)/shard_map/ppermute | solution.py:263
  31.3 11.2 %copy-start.4 = (f32[2,4,2,64,128]{4,3,2,1,0:T(8,128)S(1)}, f32[2,4,2,64,128]{4,3,2,1,0:T(8,128)}, u32[]{:S(2)}) copy-start(f32[2,4,2,64,128]{4,3,2,1,0:T(8,128)} %get-tuple-element.41) | copy-start | bytes 1572868
  33.7 23.4 %collective-permute-start.3 = (f32[2,4,2,64,128]{4,3,2,1,0:T(8,128)}, f32[2,4,2,64,128]{4,3,2,1,0:T(8,128)}, u32[]{:S(2)}, u32[]{:S(2)}) collective-permute-start(f32[2,4,2,64,128]{4,3,2,1,0:T(8,128)} %get-tuple-element.57), channel_id=1, source_target_pairs={{0,64},{1,65},{2,66},{3,67},{4,68},{5,69},{6,70},{7,71},{8,72},{9,... | collective-permute-start | bytes 1572872 | tf_op jit(solution)/shard_map/ppermute | solution.py:263
  44.7 12.5 %collective-permute-start.4 = (f32[2,4,2,64,128]{4,3,2,1,0:T(8,128)}, f32[2,4,2,64,128]{4,3,2,1,0:T(8,128)}, u32[]{:S(2)}, u32[]{:S(2)}) collective-permute-start(f32[2,4,2,64,128]{4,3,2,1,0:T(8,128)} %get-tuple-element.55), channel_id=1, source_target_pairs={{0,64},{1,65},{2,66},{3,67},{4,68},{5,69},{6,70},{7,71},{8,72},{9,... | collective-permute-start | bytes 1572872 | tf_op jit(solution)/shard_map/ppermute | solution.py:263
  57.1 4.3 %copy-start.3 = (f32[2,4,2,64,128]{4,3,2,1,0:T(8,128)S(1)}, f32[2,4,2,64,128]{4,3,2,1,0:T(8,128)}, u32[]{:S(2)}) copy-start(f32[2,4,2,64,128]{4,3,2,1,0:T(8,128)} %get-tuple-element.46) | copy-start | bytes 1572868
  57.1 35.9 %all-to-all-start.2 = ((f32[8,128,512]{2,1,0:T(8,128)}), f32[8,128,512]{2,1,0:T(8,128)S(1)}, u32[]{:S(2)}, u32[]{:S(2)}) async-start(f32[8,128,512]{2,1,0:T(8,128)} %y_levels.1), calls=%async_computation.2 | async-start | bytes 4194304 | tf_op jit(solution)/shard_map/all_to_all | solution.py:257
  61.5 3.3 %copy-start.2 = (f32[2,4,2,64,128]{4,3,2,1,0:T(8,128)S(1)}, f32[2,4,2,64,128]{4,3,2,1,0:T(8,128)}, u32[]{:S(2)}) copy-start(f32[2,4,2,64,128]{4,3,2,1,0:T(8,128)} %get-tuple-element.48) | copy-start | bytes 1572868
  63.5 6.7 %copy-start.5 = (f32[4,2,64,128]{3,2,1,0:T(8,128)S(1)}, f32[4,2,64,128]{3,2,1,0:T(8,128)}, u32[]{:S(2)}) copy-start(f32[4,2,64,128]{3,2,1,0:T(8,128)} %get-tuple-element.45) | copy-start | bytes 786436
  63.5 31.2 %collective-permute-start.6 = (f32[2,4,2,64,128]{4,3,2,1,0:T(8,128)}, f32[2,4,2,64,128]{4,3,2,1,0:T(8,128)}, u32[]{:S(2)}, u32[]{:S(2)}) collective-permute-start(f32[2,4,2,64,128]{4,3,2,1,0:T(8,128)} %pad_maximum_fusion.1), channel_id=1, source_target_pairs={{0,16},{16,0},{32,48},{48,32},{64,80},{80,64},{96,112},{112,96},{1... | collective-permute-start | bytes 1572872 | tf_op jit(solution)/shard_map/ppermute | solution.py:288
  65.9 27.2 %copy-start.1 = (f32[4,2,64,128]{3,2,1,0:T(8,128)S(1)}, f32[4,2,64,128]{3,2,1,0:T(8,128)}, u32[]{:S(2)}) copy-start(f32[4,2,64,128]{3,2,1,0:T(8,128)} %get-tuple-element.44.keep_ref) | copy-start | bytes 786436
  66.7 28.0 %collective-permute-start.7 = (f32[2,4,2,64,128]{4,3,2,1,0:T(8,128)}, f32[2,4,2,64,128]{4,3,2,1,0:T(8,128)}, u32[]{:S(2)}, u32[]{:S(2)}) collective-permute-start(f32[2,4,2,64,128]{4,3,2,1,0:T(8,128)} %pad_maximum_fusion.2), channel_id=1, source_target_pairs={{0,32},{16,48},{32,0},{48,16},{64,96},{80,112},{96,64},{112,80},{1... | collective-permute-start | bytes 1572872 | tf_op jit(solution)/shard_map/ppermute | solution.py:288
  70.0 24.7 %collective-permute-start.8 = (f32[2,4,2,64,128]{4,3,2,1,0:T(8,128)}, f32[2,4,2,64,128]{4,3,2,1,0:T(8,128)}, u32[]{:S(2)}, u32[]{:S(2)}) collective-permute-start(f32[2,4,2,64,128]{4,3,2,1,0:T(8,128)} %pad_maximum_fusion.3), channel_id=1, source_target_pairs={{0,48},{16,32},{32,16},{48,0},{64,112},{80,96},{96,80},{112,64},{1... | collective-permute-start | bytes 1572872 | tf_op jit(solution)/shard_map/ppermute | solution.py:288
  70.2 22.8 %collective-permute-start.5 = (f32[4,2,64,128]{3,2,1,0:T(8,128)S(1)}, f32[4,2,64,128]{3,2,1,0:T(8,128)S(1)}, u32[]{:S(2)}, u32[]{:S(2)}) collective-permute-start(f32[4,2,64,128]{3,2,1,0:T(8,128)S(1)} %copy-done.5), channel_id=1, source_target_pairs={{0,8},{1,9},{2,10},{3,11},{4,12},{5,13},{6,14},{7,15},{8,0},{9,1},... | collective-permute-start | bytes 786440 | tf_op jit(solution)/shard_map/ppermute | solution.py:263
